TPU v7x, 256 devices: a whole 4x4x8 slice. The times are simulated.
256 devices in a mesh: head: 4 (over y), seq: 64 (over x, z, core).
Axes of the slice: x: 4, y: 4, z: 8, core: 2. Of those that a mesh axis runs over, the one named last changes fastest.
Arguments:
- queries: bfloat16 [4, 8192], P(None, ('head', 'seq')), may hold values from -20 to 20
- key_cache: bfloat16 [4, 8, 65536, 128], P(None, 'head', 'seq'), may hold values from -16 to 16
- value_cache: bfloat16 [4, 8, 65536, 128], P(None, 'head', 'seq'), may hold values from -5 to 5
- page_list: int32 [4, 8, 256], P(None, 'head'), may hold values from 0 to 4095, as said below
- shard_counts: int32 [4, 8, 64], P(None, 'head'), may hold values from 0 to 8, as said below
- out_weight: bfloat16 [8192, 8192], P(('head', 'seq')), may hold values from -0.25 to 0.25
Outputs:
- output: bfloat16 [4, 8192], P(None, ('head', 'seq'))
- attention: bfloat16 [4, 8192], P(None, ('head', 'seq'))
- page_mass: float32 [4, 64, 4096], P(None, 'head', 'seq')
Inputs may be any that keep to these rules, and one draw needn't show every extreme that they name: With live = the sum of shard_counts[b, g, :], entries 0 to live - 1 of page_list[b, g] are distinct pages in ascending order, and exactly shard_counts[b, g, s] of them lie in pages s * 64 to (s + 1) * 64 - 1; entries from live on are padding. `shard_counts`: exactly 8 for some index s of every batch row and KV head; the sum over s is at most 256.
All inputs are finite; a program needn't handle non-finite values.
Results may differ from a plain program's by a relative error of at most 0.0052.
Values may be sent and summed in bfloat16 or wider, within the bound.
No kernel may reach another device: no remote copies, remote signals or barrier semaphores. Data moves between devices by JAX's collectives and lax.ppermute only.
A program may use at most 64 MiB of HBM per device.

v0:
```python
import math

import jax
import jax.numpy as jnp
from jax import lax
from jax.sharding import PartitionSpec as P

HQ = 64
KVH = 8
PAGE = 16
CAP = 8


NEGATIVE = -1e30


def laid_out(tiles, dim):
    tiles = jnp.moveaxis(tiles, 0, dim)
    dims = tiles.shape
    return tiles.reshape(*dims[:dim], dims[dim] * dims[dim + 1], *dims[dim + 2 :])


def copy_for_each(x, axis):
    copies = jnp.broadcast_to(x, (lax.axis_size(axis), *x.shape))
    return lax.all_to_all(copies, axis, split_axis=0, concat_axis=0, tiled=True)


def gathered_copies(x, axis, dim):
    return laid_out(copy_for_each(x, axis), dim)


def over_copies(x, axis):
    return copy_for_each(x, axis).max(axis=0)


def gathered_once(x, axis):
    leaves = jax.tree.leaves(x)
    turns = sorted(range(len(leaves)), key=lambda k: -leaves[k].size)
    width = (1, *leaves[turns[0]].shape)[-1]
    lines = [
        jnp.pad(leaves[k].reshape(-1), (0, -leaves[k].size % width)).reshape(-1, width)
        for k in turns
    ]
    both, at, found = (copy_for_each(jnp.concatenate(lines), axis), 0, {})
    for k, line in zip(turns, lines):
        slab = both[:, at : at + len(line)].reshape(len(both), -1)
        found[k] = slab[:, : leaves[k].size].reshape(-1, *leaves[k].shape)
        at += len(line)
    numbers = iter(range(len(leaves)))
    return jax.tree.map(lambda _: found[next(numbers)], x)


def folded_in_pairs(pieces, combine):
    while len(jax.tree.leaves(pieces)[0]) > 1:
        pieces = jax.vmap(combine)(
            *(jax.tree.map(lambda part: part[side::2], pieces) for side in (0, 1))
        )
    return jax.tree.map(lambda part: part[0], pieces)


def merged(x, axis, combine):
    pieces = gathered_once(x, axis)
    return folded_in_pairs(pieces, combine)


def taken_together(x, axis):
    return copy_for_each(x, axis).sum(axis=0)


def in_blocks(x, dim, count):
    before, after = (x.shape[:dim], x.shape[dim + 1 :])
    return jnp.moveaxis(x.reshape(*before, count, -1, *after), dim, 0)


def summed_on_arrival(x, axis, dim):
    count = lax.axis_size(axis)
    tiles = lax.all_to_all(in_blocks(x, dim, count), axis, 0, 0, tiled=True)
    return jnp.sum(tiles, axis=0)


def merge_pairs(earlier, later):
    new_peak = jnp.maximum(earlier[0], later[0])
    new_mass = earlier[1] * jnp.exp(earlier[0] - new_peak) + later[1] * jnp.exp(later[0] - new_peak)
    return (new_peak, new_mass)


def local(queries, key_cache, value_cache, page_list, shard_counts, out_weight):
    batch_rows, kv_local, token_count, head_dim = key_cache.shape
    group_size = HQ // KVH
    pages_local = token_count // PAGE
    shards = lax.axis_size("seq")
    shard_index = lax.axis_index("seq")
    score_scale = 1.0 / math.sqrt(head_dim)
    gathered = gathered_copies(queries, "seq", 1)
    query_heads = gathered.reshape(batch_rows, kv_local, group_size, head_dim)
    page_keys = key_cache.reshape(batch_rows, kv_local, pages_local, PAGE, head_dim)
    lower_keys = jnp.min(page_keys, axis=3).astype(jnp.float32)
    upper_keys = jnp.max(page_keys, axis=3).astype(jnp.float32)
    widened = query_heads.astype(jnp.float32)
    page_bound = (
        jnp.einsum(
            "bgjd,bgpd->bgjp",
            jnp.maximum(widened, 0.0),
            upper_keys,
            precision=lax.Precision.HIGHEST,
        )
        + jnp.einsum(
            "bgjd,bgpd->bgjp",
            jnp.minimum(widened, 0.0),
            lower_keys,
            precision=lax.Precision.HIGHEST,
        )
    ) * score_scale
    page_peak = jnp.max(page_bound, axis=3)
    shard_order = jnp.arange(shards, dtype=jnp.int32)
    offset = jnp.sum(shard_counts * (shard_order < shard_index).astype(jnp.int32), axis=2)
    own_count = jnp.sum(shard_counts * (shard_order == shard_index).astype(jnp.int32), axis=2)
    slot_ids = jnp.arange(CAP, dtype=jnp.int32)
    padded = jnp.concatenate([page_list, jnp.zeros((batch_rows, kv_local, CAP), jnp.int32)], axis=2)
    picked = jnp.take_along_axis(padded, offset[:, :, None] + slot_ids, axis=2)
    slot_valid = slot_ids[None, None, :] < own_count[:, :, None]
    local_pages = jnp.where(slot_valid, picked - shard_index * pages_local, 0)
    flat_keys = key_cache.reshape(batch_rows, kv_local, pages_local, PAGE * head_dim)
    flat_values = value_cache.reshape(batch_rows, kv_local, pages_local, PAGE * head_dim)
    chosen_keys = jnp.take_along_axis(flat_keys, local_pages[:, :, :, None], axis=2).reshape(
        batch_rows, kv_local, CAP * PAGE, head_dim
    )
    chosen_values = jnp.take_along_axis(flat_values, local_pages[:, :, :, None], axis=2).reshape(
        batch_rows, kv_local, CAP * PAGE, head_dim
    )
    live_tokens = jnp.repeat(slot_valid, PAGE, axis=2)
    scores = (
        jnp.einsum("bgjd,bgtd->bgjt", query_heads, chosen_keys, preferred_element_type=jnp.float32)
        * score_scale
    )
    masked = jnp.where(live_tokens[:, :, None, :], scores, NEGATIVE)
    local_top = jnp.max(masked, axis=3)
    global_top = over_copies(local_top, "seq")
    local_mass = jnp.sum(jnp.exp(page_bound - page_peak[..., None]), axis=3)
    page_top, page_sum = merged((page_peak, local_mass), "seq", merge_pairs)
    page_terms = jnp.exp(page_bound - page_top[..., None])
    page_mass = (page_terms / page_sum[..., None]).reshape(
        batch_rows, kv_local * group_size, pages_local
    )
    weights = jnp.where(live_tokens[:, :, None, :], jnp.exp(masked - global_top[..., None]), 0.0)
    local_totals = jnp.sum(weights, axis=3)
    unnormed = jnp.einsum(
        "bgjt,bgtd->bgjd",
        weights.astype(jnp.bfloat16),
        chosen_values,
        preferred_element_type=jnp.float32,
    )
    head_totals = taken_together(local_totals.reshape(batch_rows, kv_local * group_size), "seq")
    columns = summed_on_arrival(
        unnormed.reshape(batch_rows, kv_local * group_size * head_dim), "seq", 1
    )
    column_width = columns.shape[1]
    column_heads = (
        shard_index * column_width + jnp.arange(column_width, dtype=jnp.int32)
    ) // head_dim
    selector = (
        column_heads[:, None] == jnp.arange(kv_local * group_size, dtype=jnp.int32)[None, :]
    ).astype(jnp.float32)
    column_total = jnp.dot(head_totals, selector.T, precision=lax.Precision.HIGHEST)
    attention = (columns / column_total).astype(jnp.bfloat16)
    out_terms = jnp.dot(attention, out_weight, preferred_element_type=jnp.float32)
    halfway = summed_on_arrival(out_terms, "head", 1)
    summed = summed_on_arrival(halfway, "seq", 1)
    return (summed.astype(jnp.bfloat16), attention, page_mass)


def solution(mesh):
    return jax.shard_map(
        local,
        mesh=mesh,
        in_specs=(
            P(None, ("head", "seq")),
            P(None, "head", "seq", None),
            P(None, "head", "seq", None),
            P(None, "head", None),
            P(None, "head", None),
            P(("head", "seq"), None),
        ),
        out_specs=(P(None, ("head", "seq")), P(None, ("head", "seq")), P(None, "head", "seq")),
        check_vma=False,
    )
```

profile of v0, /device:TPU:1, one launch (start us, length us, event | category | flops | bytes accessed | tf_op | source)
XLA Modules:
  0.0 135.5 jit_solution(5380835779237507258)
XLA Ops:
  0.6 1.4 %broadcast_in_dim.67 = bf16[64,4,32]{2,1,0:T(4,128)(2,1)} broadcast(bf16[4,32]{1,0:T(4,128)(2,1)} %param.8), dimensions={1,2} | broadcast | bytes 16640 | tf_op jit(solution)/shard_map/broadcast_in_dim | solution.py:24
  2.0 13.0 %all-to-all-start = ((bf16[64,4,32]{2,1,0:T(4,128)(2,1)}), bf16[64,4,32]{2,1,0:T(4,128)(2,1)S(1)}, u32[]{:S(2)}, u32[]{:S(2)}) async-start(bf16[64,4,32]{2,1,0:T(4,128)(2,1)} %broadcast_in_dim.67), calls=%async_computation | async-start | bytes 131072 | tf_op jit(solution)/shard_map/all_to_all | solution.py:25
  15.0 4.3 %reshape.129 = bf16[4,2,64,2048]{3,2,1,0:T(8,128)(2,1)} reshape(bf16[4,2,1024,128]{3,2,1,0:T(8,128)(2,1)} %param.9) | data formatting | bytes 4194304 | tf_op jit(solution)/shard_map/reshape | solution.py:123
  19.4 2.2 %bitcast_reduce_fusion = (bf16[4,2,64,128]{3,2,1,0:T(8,128)(2,1)S(1)}, bf16[4,2,64,128]{3,2,1,0:T(8,128)(2,1)S(1)}) fusion(bf16[4,2,1024,128]{3,2,1,0:T(8,128)(2,1)S(1)} %copy-done.1), kind=kLoop, calls=%fused_computation.3 | loop fusion | flops 1966080 | bytes 2359296 | tf_op jit(solution)/shard_map/reduce_min | solution.py:97
  22.0 1.0 gather_fusion
  23.4 4.3 %reshape.131 = bf16[4,2,64,2048]{3,2,1,0:T(8,128)(2,1)} reshape(bf16[4,2,1024,128]{3,2,1,0:T(8,128)(2,1)} %param.10) | data formatting | bytes 4194304 | tf_op jit(solution)/shard_map/reshape | solution.py:124
  27.7 1.6 %gather_fusion.1 = bf16[64,2048]{1,0:T(8,128)(2,1)S(1)} fusion(bf16[4,2,64,2048]{3,2,1,0:T(8,128)(2,1)S(1)} %copy-done.2, s32[64]{0:T(128)S(1)} %reshape.159), kind=kCustom, calls=%fused_computation.clone | custom fusion | bytes 525056 | tf_op jit(solution)/shard_map/jit(take_along_axis)/gather | solution.py:125
  29.3 2.3 %gather_fusion.2 = bf16[64,2048]{1,0:T(8,128)(2,1)S(1)} fusion(bf16[4,2,64,2048]{3,2,1,0:T(8,128)(2,1)} %reshape.131, s32[64]{0:T(128)S(1)} %reshape.159), kind=kCustom, calls=%fused_computation.1.clone | custom fusion | bytes 525056 | tf_op jit(solution)/shard_map/jit(take_along_axis)/gather | solution.py:128
  32.7 0.8 broadcast_in_dim.69
  33.5 10.4 %all-to-all-start.1 = ((f32[64,4,2,8]{3,2,1,0:T(2,128)}), f32[64,4,2,8]{3,2,1,0:T(2,128)S(1)}, u32[]{:S(2)}, u32[]{:S(2)}) async-start(f32[64,4,2,8]{3,2,1,0:T(2,128)} %broadcast_in_dim.69), calls=%async_computation.1 | async-start | bytes 524288 | tf_op jit(solution)/shard_map/all_to_all | solution.py:25
  44.2 0.4 fusion.23
  44.9 0.7 reshape.173
  45.7 10.2 %all-to-all-done.1 = f32[64,4,2,8]{3,2,1,0:T(2,128)S(1)} async-done(((f32[64,4,2,8]{3,2,1,0:T(2,128)}), f32[64,4,2,8]{3,2,1,0:T(2,128)S(1)}, u32[]{:S(2)}, u32[]{:S(2)}) %all-to-all-start.1) | async-done | bytes 16416 | tf_op jit(solution)/shard_map/all_to_all | solution.py:25
  55.9 6.0 %all-to-all-start.6 = ((f32[64,1,128]{2,1,0:T(1,128)}), f32[64,1,128]{2,1,0:T(1,128)S(1)}, u32[]{:S(2)}, u32[]{:S(2)}) async-start(f32[64,1,128]{2,1,0:T(1,128)} %reshape.173), calls=%async_computation.6 | async-start | bytes 65536 | tf_op jit(solution)/shard_map/all_to_all | solution.py:25
  62.5 0.8 reshape.169
  63.5 7.7 %all-to-all-done.6 = f32[64,1,128]{2,1,0:T(1,128)S(1)} async-done(((f32[64,1,128]{2,1,0:T(1,128)}), f32[64,1,128]{2,1,0:T(1,128)S(1)}, u32[]{:S(2)}, u32[]{:S(2)}) %all-to-all-start.6) | async-done | bytes 32800 | tf_op jit(solution)/shard_map/all_to_all | solution.py:25
  71.2 0.7 broadcast_in_dim.71
  71.9 4.7 %all-to-all-start.3 = ((f32[64,4,16]{2,1,0:T(4,128)}), f32[64,4,16]{2,1,0:T(4,128)S(1)}, u32[]{:S(2)}, u32[]{:S(2)}) async-start(f32[64,4,16]{2,1,0:T(4,128)} %broadcast_in_dim.71), calls=%async_computation.3 | async-start | bytes 262144 | tf_op jit(solution)/shard_map/all_to_all | solution.py:25
  76.6 0.5 broadcast.248
  77.1 0.7 reduce.6
  78.3 0.6 slice.97
  78.9 0.6 slice.96
  79.6 0.6 slice.84
  80.2 0.6 slice.83
  80.8 0.5 slice.99
  81.3 0.5 slice.98
  81.7 0.5 slice.86
  82.2 0.5 slice.85
  82.7 0.4 slice.101
  83.1 0.4 slice.100
  83.5 0.4 slice.88
  83.9 0.4 slice.87
  84.3 0.3 slice.103
  84.9 0.3 slice.90
  85.3 0.3 slice.89
  85.6 0.3 slice.105
  87.1 10.3 %all-to-all-start.2 = ((f32[64,1,128]{2,1,0:T(1,128)}), f32[64,1,128]{2,1,0:T(1,128)S(1)}, u32[]{:S(2)}, u32[]{:S(2)}) async-start(f32[64,1,128]{2,1,0:T(1,128)} %reshape.169), calls=%async_computation.2 | async-start | bytes 65536 | tf_op jit(solution)/shard_map/all_to_all | solution.py:77
  97.5 9.1 %all-to-all-done.2 = f32[64,1,128]{2,1,0:T(1,128)S(1)} async-done(((f32[64,1,128]{2,1,0:T(1,128)}), f32[64,1,128]{2,1,0:T(1,128)S(1)}, u32[]{:S(2)}, u32[]{:S(2)}) %all-to-all-start.2) | async-done | bytes 32800 | tf_op jit(solution)/shard_map/all_to_all | solution.py:77
  106.6 0.7 reduce.4
  107.7 0.8 fusion.24
  108.6 4.1 %all-to-all-start.4 = ((f32[4,4,2048]{2,1,0:T(4,128)}), f32[4,4,2048]{2,1,0:T(4,128)S(1)}, u32[]{:S(2)}, u32[]{:S(2)}) async-start(f32[4,4,2048]{2,1,0:T(4,128)} %bitcast.8), calls=%async_computation.4 | async-start | bytes 262144 | tf_op jit(solution)/shard_map/all_to_all | solution.py:77
  112.8 4.7 %all-to-all-done.4 = f32[4,4,2048]{2,1,0:T(4,128)S(1)} async-done(((f32[4,4,2048]{2,1,0:T(4,128)}), f32[4,4,2048]{2,1,0:T(4,128)S(1)}, u32[]{:S(2)}, u32[]{:S(2)}) %all-to-all-start.4) | async-done | bytes 131104 | tf_op jit(solution)/shard_map/all_to_all | solution.py:77
  117.7 0.7 reshape.171
  118.4 6.1 %all-to-all-start.5 = ((f32[64,1,128]{2,1,0:T(1,128)}), f32[64,1,128]{2,1,0:T(1,128)S(1)}, u32[]{:S(2)}, u32[]{:S(2)}) async-start(f32[64,1,128]{2,1,0:T(1,128)} %reshape.171), calls=%async_computation.5 | async-start | bytes 65536 | tf_op jit(solution)/shard_map/all_to_all | solution.py:77
  124.6 0.7 divide_bitcast_fusion
  125.3 8.7 %all-to-all-done.5 = f32[64,1,128]{2,1,0:T(1,128)S(1)} async-done(((f32[64,1,128]{2,1,0:T(1,128)}), f32[64,1,128]{2,1,0:T(1,128)S(1)}, u32[]{:S(2)}, u32[]{:S(2)}) %all-to-all-start.5) | async-done | bytes 32800 | tf_op jit(solution)/shard_map/all_to_all | solution.py:77
  134.0 0.7 reduce.5
  134.8 0.6 reduce_sum.78
  (68 shorter events, 6.3 us)
Async XLA Ops:
  0.6 107.1 %copy-start = (bf16[32,8192]{1,0:T(8,128)(2,1)S(1)}, bf16[32,8192]{1,0:T(8,128)(2,1)}, u32[]{:S(2)}) copy-start(bf16[32,8192]{1,0:T(8,128)(2,1)} %param.13) | copy-start | bytes 1572868
  2.0 30.2 %all-to-all-start = ((bf16[64,4,32]{2,1,0:T(4,128)(2,1)}), bf16[64,4,32]{2,1,0:T(4,128)(2,1)S(1)}, u32[]{:S(2)}, u32[]{:S(2)}) async-start(bf16[64,4,32]{2,1,0:T(4,128)(2,1)} %broadcast_in_dim.67), calls=%async_computation | async-start | bytes 131072 | tf_op jit(solution)/shard_map/all_to_all | solution.py:25
  15.0 4.3 %copy-start.1 = (bf16[4,2,1024,128]{3,2,1,0:T(8,128)(2,1)S(1)}, bf16[4,2,1024,128]{3,2,1,0:T(8,128)(2,1)}, u32[]{:S(2)}) copy-start(bf16[4,2,1024,128]{3,2,1,0:T(8,128)(2,1)} %param.9) | copy-start | bytes 6291460
  19.4 2.2 %copy-start.4 = (s32[4,2,64]{2,1,0:T(2,128)S(1)}, s32[4,2,64]{2,1,0:T(2,128)}, u32[]{:S(2)}) copy-start(s32[4,2,64]{2,1,0:T(2,128)} %param.12) | copy-start | bytes 6148
  19.4 2.6 %copy-start.3 = (s32[4,2,256]{2,1,0:T(2,128)S(1)}, s32[4,2,256]{2,1,0:T(2,128)}, u32[]{:S(2)}) copy-start(s32[4,2,256]{2,1,0:T(2,128)} %param.11) | copy-start | bytes 24580
  23.4 4.3 %copy-start.2 = (bf16[4,2,64,2048]{3,2,1,0:T(8,128)(2,1)S(1)}, bf16[4,2,64,2048]{3,2,1,0:T(8,128)(2,1)}, u32[]{:S(2)}) copy-start(bf16[4,2,64,2048]{3,2,1,0:T(8,128)(2,1)} %reshape.129) | copy-start | bytes 6291460
  33.5 22.4 %all-to-all-start.1 = ((f32[64,4,2,8]{3,2,1,0:T(2,128)}), f32[64,4,2,8]{3,2,1,0:T(2,128)S(1)}, u32[]{:S(2)}, u32[]{:S(2)}) async-start(f32[64,4,2,8]{3,2,1,0:T(2,128)} %broadcast_in_dim.69), calls=%async_computation.1 | async-start | bytes 524288 | tf_op jit(solution)/shard_map/all_to_all | solution.py:25
  55.9 15.3 %all-to-all-start.6 = ((f32[64,1,128]{2,1,0:T(1,128)}), f32[64,1,128]{2,1,0:T(1,128)S(1)}, u32[]{:S(2)}, u32[]{:S(2)}) async-start(f32[64,1,128]{2,1,0:T(1,128)} %reshape.173), calls=%async_computation.6 | async-start | bytes 65536 | tf_op jit(solution)/shard_map/all_to_all | solution.py:25
  71.9 15.2 %all-to-all-start.3 = ((f32[64,4,16]{2,1,0:T(4,128)}), f32[64,4,16]{2,1,0:T(4,128)S(1)}, u32[]{:S(2)}, u32[]{:S(2)}) async-start(f32[64,4,16]{2,1,0:T(4,128)} %broadcast_in_dim.71), calls=%async_computation.3 | async-start | bytes 262144 | tf_op jit(solution)/shard_map/all_to_all | solution.py:25
  87.1 19.5 %all-to-all-start.2 = ((f32[64,1,128]{2,1,0:T(1,128)}), f32[64,1,128]{2,1,0:T(1,128)S(1)}, u32[]{:S(2)}, u32[]{:S(2)}) async-start(f32[64,1,128]{2,1,0:T(1,128)} %reshape.169), calls=%async_computation.2 | async-start | bytes 65536 | tf_op jit(solution)/shard_map/all_to_all | solution.py:77
  107.7 27.8 %copy-start.5 = (bf16[4,32]{1,0:T(4,128)(2,1)}, bf16[4,32]{1,0:T(4,128)(2,1)S(1)}, u32[]{:S(2)}) copy-start(bf16[4,32]{1,0:T(4,128)(2,1)S(1)} %fusion.3) | copy-start | bytes 772
  108.6 8.9 %all-to-all-start.4 = ((f32[4,4,2048]{2,1,0:T(4,128)}), f32[4,4,2048]{2,1,0:T(4,128)S(1)}, u32[]{:S(2)}, u32[]{:S(2)}) async-start(f32[4,4,2048]{2,1,0:T(4,128)} %bitcast.8), calls=%async_computation.4 | async-start | bytes 262144 | tf_op jit(solution)/shard_map/all_to_all | solution.py:77
  118.4 15.6 %all-to-all-start.5 = ((f32[64,1,128]{2,1,0:T(1,128)}), f32[64,1,128]{2,1,0:T(1,128)S(1)}, u32[]{:S(2)}, u32[]{:S(2)}) async-start(f32[64,1,128]{2,1,0:T(1,128)} %reshape.171), calls=%async_computation.5 | async-start | bytes 65536 | tf_op jit(solution)/shard_map/all_to_all | solution.py:77
where the time goes:
time: 136 us; the launch traced here: 135 us
  starting transfers between devices  54.6 us (40%)
  waiting for transfers between devices  40.6 us (30%)
  local copies, waits for them, and re-layouts  29.6 us (22%)
  other arithmetic  7.32 us (5%)
  matrix products  2.27 us (2%)
    all_to_all x4, starting transfers between devices, copy_for_each(): return lax.all_to_all(copies, axis, split_axis=0, concat_axis=0, tiled=True)  34.1 us
    all_to_all x3, waiting for transfers between devices, summed_on_arrival(): tiles = lax.all_to_all(in_blocks(x, dim, count), axis, 0, 0, tiled=True)  22.4 us
    all_to_all x3, starting transfers between devices, summed_on_arrival(): tiles = lax.all_to_all(in_blocks(x, dim, count), axis, 0, 0, tiled=True)  20.5 us
    all_to_all x4, waiting for transfers between devices, copy_for_each(): return lax.all_to_all(copies, axis, split_axis=0, concat_axis=0, tiled=True)  18.1 us
    slice x20, local copies, waits for them, and re-layouts, folded_in_pairs(): part[side::2]  8.28 us
    reshape x1, local copies, waits for them, and re-layouts, local(): value_cache.reshape(batch_rows, kv_local, pages_local, PAGE * head_dim)  4.33 us
    reshape x1, local copies, waits for them, and re-layouts, local(): key_cache.reshape(batch_rows, kv_local, pages_local, PAGE * head_dim)  4.32 us
    unnamed x21, local copies, waits for them, and re-layouts  2.92 us
  transfers between devices with their start and end apart: 7, of which 6 were waited for; matrix products, arithmetic and copies ran while one was open for 23% of the time, Pallas kernels for 0%

commit v1 on v0

v1 whole, which is shorter than its diff:
```python
import functools
import math

import jax
import jax.numpy as jnp
from jax import lax
from jax.experimental import pallas as pl
from jax.experimental.pallas import tpu as pltpu
from jax.sharding import PartitionSpec as P

HQ = 64
KVH = 8
HD = 128
PAGE = 16
CAP = 8
LANES = 128
NEGATIVE = -1e30
SCALE = 1.0 / math.sqrt(HD)

VMEM = pl.BlockSpec(memory_space=pltpu.VMEM)
SMEM = pl.BlockSpec(memory_space=pltpu.SMEM)


def block_lanes(shape, width):
    return lax.broadcasted_iota(jnp.int32, shape, 1) // width


def spread_kernel(copies, query_ref, out_ref):
    rows = query_ref[...].astype(jnp.float32)
    line = jnp.concatenate([rows[b : b + 1, :] for b in range(rows.shape[0])], axis=1)
    out_ref[...] = jnp.broadcast_to(line, (copies, LANES))


def prepare_kernel(counts_ref, pages_ref, key_ref, value_ref, ends_ref, keys_out, values_out):
    batch, groups, tokens, dim = key_ref.shape
    pages = tokens // PAGE
    shard = lax.axis_index("seq")
    pairs = [(b, g) for b in range(batch) for g in range(groups)]

    def before(s, sums):
        return tuple(t + counts_ref[b, g, s] for t, (b, g) in zip(sums, pairs))

    offsets = lax.fori_loop(0, shard, before, (jnp.int32(0),) * len(pairs))
    for n, (b, g) in enumerate(pairs):
        count = counts_ref[b, g, shard]
        for slot in range(CAP):
            at = jnp.minimum(offsets[n] + slot, pages_ref.shape[2] - 1)
            page = jnp.where(slot < count, pages_ref[b, g, at] - shard * pages, 0)
            page = jnp.clip(page, 0, pages - 1)
            start = pl.multiple_of(page * PAGE, PAGE)
            keys_out[n, slot * PAGE : (slot + 1) * PAGE, :] = key_ref[b, g, pl.ds(start, PAGE), :]
            values_out[n, slot * PAGE : (slot + 1) * PAGE, :] = value_ref[b, g, pl.ds(start, PAGE), :]
        paged = key_ref[b, g].reshape(pages, PAGE, dim)
        ends_ref[n, :, :dim] = jnp.max(paged, axis=1)
        ends_ref[n, :, dim:] = jnp.min(paged, axis=1)


def scores_kernel(counts_ref, query_ref, ends_ref, keys_ref, values_ref, part_ref, bound_ref):
    batch, groups, _ = counts_ref.shape
    heads = query_ref.shape[0] // 4
    group = heads // groups
    width = LANES // 4
    shard = lax.axis_index("seq")
    quarters = [query_ref[pl.ds(q, heads, stride=4), :] for q in range(4)]
    lane_block = block_lanes((heads, LANES), width)

    def rows_of(b):
        found = jnp.zeros((heads, LANES), jnp.float32)
        for q in range(4):
            shift = (q - b) * width % LANES
            moved = pltpu.roll(quarters[q], shift, 1) if shift else quarters[q]
            found = jnp.where(lane_block == q, moved, found)
        return found

    lanes = lax.broadcasted_iota(jnp.int32, (group, LANES), 1)
    subs = lax.broadcasted_iota(jnp.int32, (group, LANES), 0)
    page_row = jnp.zeros((group, LANES), jnp.float32)
    head_rows = [jnp.zeros((group, LANES), jnp.float32) for _ in range(groups)]
    mixed = []
    contract = (((1,), (1,)), ((), ()))
    for b in range(batch):
        rows = rows_of(b)
        parts = []
        for g in range(groups):
            n = b * groups + g
            query = rows[g * group : (g + 1) * group]
            signed = jnp.concatenate([jnp.maximum(query, 0.0), jnp.minimum(query, 0.0)], axis=1)
            bound = SCALE * lax.dot_general(
                signed.astype(jnp.bfloat16), ends_ref[n], contract, preferred_element_type=jnp.float32
            )
            bound_ref[b, g * group : (g + 1) * group, :] = bound
            peak = jnp.max(bound, axis=1, keepdims=True)
            mass = jnp.sum(jnp.exp(bound - peak), axis=1, keepdims=True)
            page_row = jnp.where(lanes == subs * (batch * groups) + n, peak + jnp.log(mass), page_row)
            scores = SCALE * lax.dot_general(
                query.astype(jnp.bfloat16), keys_ref[n], contract, preferred_element_type=jnp.float32
            )
            live = lanes // PAGE < counts_ref[b, g, shard]
            scores = jnp.where(live, scores, NEGATIVE)
            top = jnp.max(scores, axis=1, keepdims=True)
            weights = jnp.where(live, jnp.exp(scores - top), 0.0)
            total = jnp.maximum(jnp.sum(weights, axis=1, keepdims=True), 1e-30)
            unnormed = jnp.dot(
                weights.astype(jnp.bfloat16), values_ref[n], preferred_element_type=jnp.float32
            )
            parts.append(unnormed / total)
            head_rows[g] = jnp.where(
                lanes == LANES // 2 + b, top + jnp.log(total), head_rows[g]
            )
        mixed.append(jnp.concatenate(parts, axis=0))
    page_line = jnp.sum(page_row, axis=0, keepdims=True)
    seconds = jnp.concatenate(head_rows, axis=0) + page_line
    for q in range(4):
        line = jnp.zeros((heads, LANES), jnp.float32)
        for b in range(batch):
            shift = (b - q) * width % LANES
            moved = pltpu.roll(mixed[b], shift, 1) if shift else mixed[b]
            line = jnp.where(lane_block == b, moved, line)
        part_ref[pl.ds(2 * q, heads, stride=8), :] = line
        part_ref[pl.ds(2 * q + 1, heads, stride=8), :] = seconds


def project_kernel(part_ref, weight_ref, attention_ref, out_ref):
    shards = part_ref.shape[0] // 2
    width = LANES // 4
    values = part_ref[pl.ds(0, shards, stride=2), :]
    logs = part_ref[pl.ds(1, shards, stride=2), :]
    shares = jnp.exp(logs - jnp.max(logs, axis=0, keepdims=True))
    block = block_lanes((shards, LANES), width)
    spread = jnp.zeros((shards, LANES), jnp.float32)
    for b in range(4):
        at = LANES // 2 + b
        spread = jnp.where(block == b, shares[:, at : at + 1], spread)
    line = jnp.sum(spread * values, axis=0, keepdims=True) / jnp.sum(spread, axis=0, keepdims=True)
    for b in range(4):
        attention_ref[b : b + 1, :] = line[:, b * width : (b + 1) * width].astype(jnp.bfloat16)
    line = line.astype(jnp.bfloat16).astype(jnp.float32)
    lanes = lax.broadcasted_iota(jnp.int32, (width, LANES), 1)
    subs = lax.broadcasted_iota(jnp.int32, (width, LANES), 0)
    picked = jnp.where(lanes % width == subs, line, 0.0).astype(jnp.bfloat16)
    same = (
        lax.broadcasted_iota(jnp.int32, (LANES, LANES), 0) // width
        == block_lanes((LANES, LANES), width)
    )
    turned = jnp.dot(
        picked, jnp.where(same, 1.0, 0.0).astype(jnp.bfloat16), preferred_element_type=jnp.float32
    )
    diagonal = lanes % width == subs
    wide = jnp.concatenate(
        [jnp.where(diagonal, turned[k : k + 1, :], 0.0).astype(jnp.bfloat16) for k in range(width)],
        axis=0,
    )
    out_ref[...] = jnp.dot(weight_ref[...], wide, preferred_element_type=jnp.float32)


def mass_kernel(part_ref, bound_ref, mass_ref):
    batch, heads, pages = bound_ref.shape
    shards = part_ref.shape[0] // 2
    group = HQ // KVH
    groups = heads // group
    logs = part_ref[pl.ds(1, shards, stride=2), :]
    peak = jnp.max(logs, axis=0, keepdims=True)
    line = peak + jnp.log(jnp.sum(jnp.exp(logs - peak), axis=0, keepdims=True))
    lanes = lax.broadcasted_iota(jnp.int32, (group, LANES), 1)
    subs = lax.broadcasted_iota(jnp.int32, (group, LANES), 0)
    for b in range(batch):
        for g in range(groups):
            n = b * groups + g
            column = jnp.sum(
                jnp.where(lanes == subs * (batch * groups) + n, line, 0.0), axis=1, keepdims=True
            )
            rows = slice(g * group, (g + 1) * group)
            mass_ref[b, rows, :] = jnp.exp(bound_ref[b, rows, :] - column)


def total_kernel(width, terms_ref, out_ref):
    line = jnp.sum(terms_ref[...], axis=0, keepdims=True)
    for b in range(out_ref.shape[0]):
        out_ref[b : b + 1, :] = line[:, b * width : (b + 1) * width].astype(out_ref.dtype)


def call(kernel, out_shape, args, specs, nbytes, flops=0):
    many = isinstance(out_shape, tuple)
    return pl.pallas_call(
        kernel,
        out_shape=out_shape,
        in_specs=specs,
        out_specs=tuple(VMEM for _ in out_shape) if many else VMEM,
        compiler_params=pltpu.CompilerParams(vmem_limit_bytes=32 * 1024 * 1024),
        cost_estimate=pl.CostEstimate(flops=flops, bytes_accessed=nbytes, transcendentals=0),
    )(*args)


def exchanged(x, axis):
    rows = lax.axis_size(axis)
    sent = x.reshape(rows, x.shape[0] // rows, x.shape[1])
    return lax.all_to_all(sent, axis, 0, 0, tiled=True).reshape(x.shape)


def local(queries, key_cache, value_cache, page_list, shard_counts, out_weight):
    batch, groups, tokens, dim = key_cache.shape
    pages = tokens // PAGE
    shards = lax.axis_size("seq")
    devices = lax.axis_size("head") * shards
    pairs = batch * groups
    heads = groups * (HQ // KVH)
    width = queries.shape[1]
    f32, bf16 = jnp.float32, jnp.bfloat16
    S = jax.ShapeDtypeStruct

    sent = call(functools.partial(spread_kernel, shards), S((shards, LANES), f32), (queries,), [VMEM], 1 << 16)
    ends, keys, values = call(
        prepare_kernel,
        (S((pairs, pages, 2 * dim), bf16), S((pairs, CAP * PAGE, dim), bf16), S((pairs, CAP * PAGE, dim), bf16)),
        (shard_counts, page_list, key_cache, value_cache),
        [SMEM, SMEM, VMEM, VMEM],
        1 << 23,
    )
    gathered = exchanged(sent, "seq")
    weight = jnp.transpose(out_weight.reshape(width, devices, width), (1, 0, 2)).reshape(devices, width * width)
    parts, bound = call(
        scores_kernel,
        (S((2 * shards, LANES), f32), S((batch, heads, pages), f32)),
        (shard_counts, gathered, ends, keys, values),
        [SMEM, VMEM, VMEM, VMEM, VMEM],
        1 << 20,
    )
    arrived = exchanged(parts, "seq")
    attention, terms = call(
        project_kernel,
        (S((batch, width), bf16), S((devices, LANES), f32)),
        (arrived, weight),
        [VMEM, VMEM],
        1 << 20,
    )
    page_mass = call(mass_kernel, S((batch, heads, pages), f32), (arrived, bound), [VMEM, VMEM], 1 << 18)
    landed = exchanged(terms, ("head", "seq"))
    output = call(functools.partial(total_kernel, width), S((batch, width), bf16), (landed,), [VMEM], 1 << 17)
    return (output, attention, page_mass)


def solution(mesh):
    return jax.shard_map(
        local,
        mesh=mesh,
        in_specs=(
            P(None, ("head", "seq")),
            P(None, "head", "seq", None),
            P(None, "head", "seq", None),
            P(None, "head", None),
            P(None, "head", None),
            P(("head", "seq"), None),
        ),
        out_specs=(P(None, ("head", "seq")), P(None, ("head", "seq")), P(None, "head", "seq")),
        check_vma=False,
    )
```

time: 136 us -> 67 us (0.49)
  starting transfers between devices: 54.6 us -> 28.8 us
  local copies, waits for them, and re-layouts: 29.6 us -> 7.88 us
  waiting for transfers between devices: 40.6 us -> 21.5 us
  Pallas kernels: 0 us -> 7.75 us
  other arithmetic: 7.32 us -> 0 us
  matrix products: 2.27 us -> 0 us
    all_to_all x7 -> x3, starting transfers between devices: 54.6 us -> 28.8 us  [exchanged(): return lax.all_to_all(sent, axis, 0, 0, tiled=True).reshape(x.shape)]
    all_to_all x7 -> x3, waiting for transfers between devices: 40.6 us -> 21.5 us  [exchanged(): return lax.all_to_all(sent, axis, 0, 0, tiled=True).reshape(x.shape)]
    slice x21 -> x0, local copies, waits for them, and re-layouts: 8.41 us -> none  [the longest x20 8.28 us: folded_in_pairs(): part[side::2]]
    pallas_call x0 -> x6, Pallas kernels: none -> 7.75 us  [call(): pl.pallas_call(kernel, out_shape=out_shape, in_specs=specs, out_specs=tup...]
    reshape x6 -> x2, local copies, waits for them, and re-layouts: 9.08 us -> 1.84 us  [the longest x1 1.64 us: local(): out_weight.reshape(width, devices, width)]
    gather x6 -> x0, local copies, waits for them, and re-layouts: 5.13 us -> none  [the longest x1 2.31 us: local(): jnp.take_along_axis(flat_values, local_pages[:, :, :, None], axis=2)]
    broadcast_in_dim x6 -> x0, local copies, waits for them, and re-layouts: 3 us -> none  [the longest x3 2.82 us: copy_for_each(): copies = jnp.broadcast_to(x, (lax.axis_size(axis), *x.shape))]
    unnamed x21 -> x14, local copies, waits for them, and re-layouts: 2.92 us -> 5.24 us
  transfers between devices with their start and end apart: 7 -> 3, of which waited for: 6 -> 3; matrix products, arithmetic and copies ran while one was open for 23% -> 4% of each run, Pallas kernels for 0% -> 5%
where the time goes in v1:
time: 67 us; the launch traced here: 66.6 us
  starting transfers between devices  28.8 us (43%)
  waiting for transfers between devices  21.5 us (32%)
  local copies, waits for them, and re-layouts  7.88 us (12%)
  Pallas kernels  7.75 us (12%)
  between operations  0.71 us (1%)
    all_to_all x3, starting transfers between devices, exchanged(): return lax.all_to_all(sent, axis, 0, 0, tiled=True).reshape(x.shape)  28.8 us
    all_to_all x3, waiting for transfers between devices, exchanged(): return lax.all_to_all(sent, axis, 0, 0, tiled=True).reshape(x.shape)  21.5 us
    pallas_call x6, Pallas kernels, call(): pl.pallas_call(kernel, out_shape=out_shape, in_specs=specs, out_specs=tup...  7.75 us
    unnamed x14, local copies, waits for them, and re-layouts  5.24 us
    reshape x1, local copies, waits for them, and re-layouts, local(): out_weight.reshape(width, devices, width)  1.64 us
  transfers between devices with their start and end apart: 3, of which 3 were waited for; matrix products, arithmetic and copies ran while one was open for 4% of the time, Pallas kernels for 5%

profile of v1, /device:TPU:1, one launch (start us, length us, event | category | flops | bytes accessed | tf_op | source)
XLA Modules:
  0.0 66.6 jit_solution(15252904558908594000)
XLA Ops:
  0.6 0.0 copy-start.5
  0.6 0.7 %copy-done.5 = bf16[4,32]{1,0:T(4,128)(2,1)S(1)} copy-done((bf16[4,32]{1,0:T(4,128)(2,1)S(1)}, bf16[4,32]{1,0:T(4,128)(2,1)}, u32[]{:S(2)}) %copy-start.5) | copy-done | bytes 280
  1.3 0.7 %shard_map.85 = f32[64,128]{1,0:T(8,128)} custom-call(bf16[4,32]{1,0:T(4,128)(2,1)S(1)} %copy-done.5), custom_call_target="tpu_custom_call" | custom-call | bytes 65536 | tf_op jit(solution)/shard_map/pallas_call | solution.py:184
  2.0 13.0 %all-to-all-start = ((f32[64,1,128]{2,1,0:T(1,128)}), f32[64,1,128]{2,1,0:T(1,128)S(1)}, u32[]{:S(2)}, u32[]{:S(2)}) async-start(f32[64,1,128]{2,1,0:T(1,128)} %bitcast.1), calls=%async_computation | async-start | bytes 65536 | tf_op jit(solution)/shard_map/all_to_all | solution.py:197
  15.0 0.0 copy-start
  15.0 1.6 %copy-done = bf16[4,2,1024,128]{3,2,1,0:T(8,128)(2,1)S(1)} copy-done((bf16[4,2,1024,128]{3,2,1,0:T(8,128)(2,1)S(1)}, bf16[4,2,1024,128]{3,2,1,0:T(8,128)(2,1)}, u32[]{:S(2)}) %copy-start) | copy-done | bytes 2097176
  16.6 0.0 copy-start.1
  16.6 1.6 %copy-done.1 = bf16[4,2,1024,128]{3,2,1,0:T(8,128)(2,1)S(1)} copy-done((bf16[4,2,1024,128]{3,2,1,0:T(8,128)(2,1)S(1)}, bf16[4,2,1024,128]{3,2,1,0:T(8,128)(2,1)}, u32[]{:S(2)}) %copy-start.1) | copy-done | bytes 2097176
  18.2 0.0 copy-start.2
  18.2 0.7 %copy-done.2 = s32[4,2,64]{2,1,0:T(2,128)S(1)} copy-done((s32[4,2,64]{2,1,0:T(2,128)S(1)}, s32[4,2,64]{2,1,0:T(2,128)}, u32[]{:S(2)}) %copy-start.2) | copy-done | bytes 2072
  18.9 0.0 copy-start.4
  18.9 0.7 %copy-done.4 = s32[4,2,256]{2,1,0:T(2,128)S(1)} copy-done((s32[4,2,256]{2,1,0:T(2,128)S(1)}, s32[4,2,256]{2,1,0:T(2,128)}, u32[]{:S(2)}) %copy-start.4) | copy-done | bytes 8216
  19.6 0.0 copy-start.3
  19.6 0.0 copy-start.6
  19.6 2.4 %shard_map.86 = (bf16[8,64,256]{2,1,0:T(8,128)(2,1)S(1)}, bf16[8,128,128]{2,1,0:T(8,128)(2,1)S(1)}, bf16[8,128,128]{2,1,0:T(8,128)(2,1)S(1)}) custom-call(s32[4,2,64]{2,1,0:T(2,128)S(1)} %copy-done.2, s32[4,2,256]{2,1,0:T(2,128)S(1)} %copy-done.4, bf16[4,2,1024,128]{3,2,1,0:T(8,128)(2,1)S(1)} %copy-done, bf16[4,2,1024,128]{3,2,1,0:T(8,128)(2,1)S(1)} %copy-done.1), custom_call_target="tpu_custom_call" | custom-call | bytes 8388608 | tf_op jit(solution)/shard_map/pallas_call | solution.py:184
  22.0 2.2 %all-to-all-done = f32[64,1,128]{2,1,0:T(1,128)S(1)} async-done(((f32[64,1,128]{2,1,0:T(1,128)}), f32[64,1,128]{2,1,0:T(1,128)S(1)}, u32[]{:S(2)}, u32[]{:S(2)}) %all-to-all-start) | async-done | bytes 32800 | tf_op jit(solution)/shard_map/all_to_all | solution.py:197
  24.2 0.0 copy-done.3
  24.2 2.0 %shard_map.87 = (f32[128,128]{1,0:T(8,128)}, f32[4,16,64]{2,1,0:T(8,128)S(1)}) custom-call(s32[4,2,64]{2,1,0:T(2,128)S(1)} %copy-done.3, f32[64,128]{1,0:T(8,128)S(1)} %bitcast.15, bf16[8,64,256]{2,1,0:T(8,128)(2,1)S(1)} %get-tuple-element.10.ends_ref, bf16[8,128,128]{2,1,0:T(8,128)(2,1)S(1)} %get-tuple-element.11.keys_ref, ...), custom_call_target="tpu_custom_call" | custom-call | bytes 1048576 | tf_op jit(solution)/shard_map/pallas_call | solution.py:184
  26.2 9.1 %all-to-all-start.1 = ((f32[64,2,128]{2,1,0:T(2,128)}), f32[64,2,128]{2,1,0:T(2,128)S(1)}, u32[]{:S(2)}, u32[]{:S(2)}) async-start(f32[64,2,128]{2,1,0:T(2,128)} %bitcast.3), calls=%async_computation.1 | async-start | bytes 131072 | tf_op jit(solution)/shard_map/all_to_all | solution.py:197
  35.3 0.0 copy-done.6
  35.3 1.6 %reshape.34 = bf16[32,256,32]{2,1,0:T(8,128)(2,1)S(1)} reshape(bf16[32,8192]{1,0:T(8,128)(2,1)S(1)} %copy-done.6) | data formatting | bytes 1048576 | tf_op jit(solution)/shard_map/reshape | solution.py:220
  37.0 0.8 %copy.13 = bf16[256,32,32]{0,2,1:T(8,128)(2,1)S(1)} copy(bf16[256,32,32]{2,0,1:T(8,128)(2,1)S(1)} %bitcast.16) | data formatting | bytes 1048576 | tf_op jit(solution)/shard_map/transpose | solution.py:220
  37.8 0.2 copy.14.weight_ref
  38.0 7.1 %all-to-all-done.1 = f32[64,2,128]{2,1,0:T(2,128)S(1)} async-done(((f32[64,2,128]{2,1,0:T(2,128)}), f32[64,2,128]{2,1,0:T(2,128)S(1)}, u32[]{:S(2)}, u32[]{:S(2)}) %all-to-all-start.1) | async-done | bytes 65568 | tf_op jit(solution)/shard_map/all_to_all | solution.py:197
  45.1 1.2 %shard_map.88 = (bf16[4,32]{1,0:T(4,128)(2,1)}, f32[256,128]{1,0:T(8,128)}) custom-call(f32[128,128]{1,0:T(8,128)S(1)} %bitcast.12, bf16[256,1024]{1,0:T(8,128)(2,1)S(1)} %copy.14.weight_ref), custom_call_target="tpu_custom_call" | custom-call | bytes 1048576 | tf_op jit(solution)/shard_map/pallas_call | solution.py:184
  46.3 6.7 %all-to-all-start.2 = ((f32[256,1,128]{2,1,0:T(1,128)}), f32[256,1,128]{2,1,0:T(1,128)S(1)}, u32[]{:S(2)}, u32[]{:S(2)}) async-start(f32[256,1,128]{2,1,0:T(1,128)} %bitcast.8), calls=%async_computation.2 | async-start | bytes 262144 | tf_op jit(solution)/shard_map/all_to_all | solution.py:197
  53.1 0.7 %shard_map.90 = f32[4,16,64]{2,1,0:T(8,128)} custom-call(f32[128,128]{1,0:T(8,128)S(1)} %bitcast.13, f32[4,16,64]{2,1,0:T(8,128)S(1)} %get-tuple-element.16.bound_ref), custom_call_target="tpu_custom_call" | custom-call | bytes 262144 | tf_op jit(solution)/shard_map/pallas_call | solution.py:184
  53.8 12.1 %all-to-all-done.2 = f32[256,1,128]{2,1,0:T(1,128)S(1)} async-done(((f32[256,1,128]{2,1,0:T(1,128)}), f32[256,1,128]{2,1,0:T(1,128)S(1)}, u32[]{:S(2)}, u32[]{:S(2)}) %all-to-all-start.2) | async-done | bytes 131104 | tf_op jit(solution)/shard_map/all_to_all | solution.py:197
  65.9 0.7 %shard_map.89 = bf16[4,32]{1,0:T(4,128)(2,1)} custom-call(f32[256,128]{1,0:T(8,128)S(1)} %bitcast.14), custom_call_target="tpu_custom_call" | custom-call | bytes 131072 | tf_op jit(solution)/shard_map/pallas_call | solution.py:184
Async XLA Ops:
  0.6 0.7 %copy-start.5 = (bf16[4,32]{1,0:T(4,128)(2,1)S(1)}, bf16[4,32]{1,0:T(4,128)(2,1)}, u32[]{:S(2)}) copy-start(bf16[4,32]{1,0:T(4,128)(2,1)} %query_ref.1) | copy-start | bytes 772
  2.0 22.2 %all-to-all-start = ((f32[64,1,128]{2,1,0:T(1,128)}), f32[64,1,128]{2,1,0:T(1,128)S(1)}, u32[]{:S(2)}, u32[]{:S(2)}) async-start(f32[64,1,128]{2,1,0:T(1,128)} %bitcast.1), calls=%async_computation | async-start | bytes 65536 | tf_op jit(solution)/shard_map/all_to_all | solution.py:197
  15.0 1.6 %copy-start = (bf16[4,2,1024,128]{3,2,1,0:T(8,128)(2,1)S(1)}, bf16[4,2,1024,128]{3,2,1,0:T(8,128)(2,1)}, u32[]{:S(2)}) copy-start(bf16[4,2,1024,128]{3,2,1,0:T(8,128)(2,1)} %key_ref.1) | copy-start | bytes 6291460
  16.6 1.6 %copy-start.1 = (bf16[4,2,1024,128]{3,2,1,0:T(8,128)(2,1)S(1)}, bf16[4,2,1024,128]{3,2,1,0:T(8,128)(2,1)}, u32[]{:S(2)}) copy-start(bf16[4,2,1024,128]{3,2,1,0:T(8,128)(2,1)} %value_ref.1) | copy-start | bytes 6291460
  18.2 0.7 %copy-start.2 = (s32[4,2,64]{2,1,0:T(2,128)S(1)}, s32[4,2,64]{2,1,0:T(2,128)}, u32[]{:S(2)}) copy-start(s32[4,2,64]{2,1,0:T(2,128)} %counts_ref.3) | copy-start | bytes 6148
  18.9 0.7 %copy-start.4 = (s32[4,2,256]{2,1,0:T(2,128)S(1)}, s32[4,2,256]{2,1,0:T(2,128)}, u32[]{:S(2)}) copy-start(s32[4,2,256]{2,1,0:T(2,128)} %pages_ref.1) | copy-start | bytes 24580
  19.6 4.6 %copy-start.3 = (s32[4,2,64]{2,1,0:T(2,128)S(1)}, s32[4,2,64]{2,1,0:T(2,128)}, u32[]{:S(2)}) copy-start(s32[4,2,64]{2,1,0:T(2,128)} %counts_ref.3) | copy-start | bytes 6148
  19.6 15.8 %copy-start.6 = (bf16[32,8192]{1,0:T(8,128)(2,1)S(1)}, bf16[32,8192]{1,0:T(8,128)(2,1)}, u32[]{:S(2)}) copy-start(bf16[32,8192]{1,0:T(8,128)(2,1)} %param.11) | copy-start | bytes 1572868
  26.2 18.9 %all-to-all-start.1 = ((f32[64,2,128]{2,1,0:T(2,128)}), f32[64,2,128]{2,1,0:T(2,128)S(1)}, u32[]{:S(2)}, u32[]{:S(2)}) async-start(f32[64,2,128]{2,1,0:T(2,128)} %bitcast.3), calls=%async_computation.1 | async-start | bytes 131072 | tf_op jit(solution)/shard_map/all_to_all | solution.py:197
  46.3 19.6 %all-to-all-start.2 = ((f32[256,1,128]{2,1,0:T(1,128)}), f32[256,1,128]{2,1,0:T(1,128)S(1)}, u32[]{:S(2)}, u32[]{:S(2)}) async-start(f32[256,1,128]{2,1,0:T(1,128)} %bitcast.8), calls=%async_computation.2 | async-start | bytes 262144 | tf_op jit(solution)/shard_map/all_to_all | solution.py:197

commit v2 on v1

--- a/solution.py
+++ b/solution.py
@@ -18,7 +18,7 @@
 SCALE = 1.0 / math.sqrt(HD)
 
 VMEM = pl.BlockSpec(memory_space=pltpu.VMEM)
-SMEM = pl.BlockSpec(memory_space=pltpu.SMEM)
+HBM = pl.BlockSpec(memory_space=pltpu.HBM)
 
 
 def block_lanes(shape, width):
@@ -31,36 +31,63 @@
     out_ref[...] = jnp.broadcast_to(line, (copies, LANES))
 
 
-def prepare_kernel(counts_ref, pages_ref, key_ref, value_ref, ends_ref, keys_out, values_out):
-    batch, groups, tokens, dim = key_ref.shape
+def prepare_kernel(
+    counts_hbm, pages_hbm, key_hbm, value_hbm,
+    live_ref, ends_ref, keys_out, values_out,
+    counts_ref, pages_ref, key_ref, value_ref, list_sems, key_sems, value_sems,
+):
+    batch, groups, tokens, dim = key_hbm.shape
     pages = tokens // PAGE
     shard = lax.axis_index("seq")
     pairs = [(b, g) for b in range(batch) for g in range(groups)]
-
-    def before(s, sums):
-        return tuple(t + counts_ref[b, g, s] for t, (b, g) in zip(sums, pairs))
-
-    offsets = lax.fori_loop(0, shard, before, (jnp.int32(0),) * len(pairs))
+    lists = [
+        pltpu.make_async_copy(counts_hbm, counts_ref, list_sems.at[0]),
+        pltpu.make_async_copy(pages_hbm, pages_ref, list_sems.at[1]),
+    ]
+    key_copies = [
+        pltpu.make_async_copy(key_hbm.at[b, g], key_ref.at[n], key_sems.at[n])
+        for n, (b, g) in enumerate(pairs)
+    ]
+    value_copies = [
+        pltpu.make_async_copy(value_hbm.at[b, g], value_ref.at[n], value_sems.at[n])
+        for n, (b, g) in enumerate(pairs)
+    ]
+    for copy in lists + key_copies + value_copies:
+        copy.start()
+    for copy in lists:
+        copy.wait()
+    chosen = []
     for n, (b, g) in enumerate(pairs):
-        count = counts_ref[b, g, shard]
+        counts = counts_ref[b, g : g + 1, :]
+        slots = lax.broadcasted_iota(jnp.int32, counts.shape, 1)
+        offset = jnp.sum(jnp.where(slots < shard, counts, 0))
+        count = jnp.sum(jnp.where(slots == shard, counts, 0), axis=1, keepdims=True)
+        lanes = lax.broadcasted_iota(jnp.int32, (1, LANES), 1)
+        live_ref[n : n + 1, :] = jnp.where(lanes // PAGE < count, 1.0, 0.0)
+        starts = []
         for slot in range(CAP):
-            at = jnp.minimum(offsets[n] + slot, pages_ref.shape[2] - 1)
-            page = jnp.where(slot < count, pages_ref[b, g, at] - shard * pages, 0)
-            page = jnp.clip(page, 0, pages - 1)
-            start = pl.multiple_of(page * PAGE, PAGE)
-            keys_out[n, slot * PAGE : (slot + 1) * PAGE, :] = key_ref[b, g, pl.ds(start, PAGE), :]
-            values_out[n, slot * PAGE : (slot + 1) * PAGE, :] = value_ref[b, g, pl.ds(start, PAGE), :]
-        paged = key_ref[b, g].reshape(pages, PAGE, dim)
+            at = jnp.minimum(offset + slot, pages_ref.shape[2] - 1)
+            page = jnp.clip(pages_ref[b, g, at] - shard * pages, 0, pages - 1)
+            starts.append(pl.multiple_of(page * PAGE, PAGE))
+        chosen.append(starts)
+    for n in range(len(pairs)):
+        key_copies[n].wait()
+        paged = key_ref[n].reshape(pages, PAGE, dim)
         ends_ref[n, :, :dim] = jnp.max(paged, axis=1)
         ends_ref[n, :, dim:] = jnp.min(paged, axis=1)
-
-
-def scores_kernel(counts_ref, query_ref, ends_ref, keys_ref, values_ref, part_ref, bound_ref):
-    batch, groups, _ = counts_ref.shape
-    heads = query_ref.shape[0] // 4
+        for slot in range(CAP):
+            keys_out[n, slot * PAGE : (slot + 1) * PAGE, :] = key_ref[n, pl.ds(chosen[n][slot], PAGE), :]
+    for n in range(len(pairs)):
+        value_copies[n].wait()
+        for slot in range(CAP):
+            values_out[n, slot * PAGE : (slot + 1) * PAGE, :] = value_ref[n, pl.ds(chosen[n][slot], PAGE), :]
+
+
+def scores_kernel(live_ref, query_ref, ends_ref, keys_ref, values_ref, part_ref, bound_ref):
+    batch, heads, _ = bound_ref.shape
+    groups = live_ref.shape[0] // batch
     group = heads // groups
     width = LANES // 4
-    shard = lax.axis_index("seq")
     quarters = [query_ref[pl.ds(q, heads, stride=4), :] for q in range(4)]
     lane_block = block_lanes((heads, LANES), width)
 
@@ -95,7 +122,7 @@
             scores = SCALE * lax.dot_general(
                 query.astype(jnp.bfloat16), keys_ref[n], contract, preferred_element_type=jnp.float32
             )
-            live = lanes // PAGE < counts_ref[b, g, shard]
+            live = live_ref[n : n + 1, :] > 0.0
             scores = jnp.where(live, scores, NEGATIVE)
             top = jnp.max(scores, axis=1, keepdims=True)
             weights = jnp.where(live, jnp.exp(scores - top), 0.0)
@@ -179,15 +206,16 @@
         out_ref[b : b + 1, :] = line[:, b * width : (b + 1) * width].astype(out_ref.dtype)
 
 
-def call(kernel, out_shape, args, specs, nbytes, flops=0):
+def call(kernel, out_shape, args, specs, nbytes, scratch=(), limit=32):
     many = isinstance(out_shape, tuple)
     return pl.pallas_call(
         kernel,
         out_shape=out_shape,
         in_specs=specs,
         out_specs=tuple(VMEM for _ in out_shape) if many else VMEM,
-        compiler_params=pltpu.CompilerParams(vmem_limit_bytes=32 * 1024 * 1024),
-        cost_estimate=pl.CostEstimate(flops=flops, bytes_accessed=nbytes, transcendentals=0),
+        scratch_shapes=list(scratch),
+        compiler_params=pltpu.CompilerParams(vmem_limit_bytes=limit << 20),
+        cost_estimate=pl.CostEstimate(flops=0, bytes_accessed=nbytes, transcendentals=0),
     )(*args)
 
 
@@ -208,21 +236,42 @@
     f32, bf16 = jnp.float32, jnp.bfloat16
     S = jax.ShapeDtypeStruct
 
-    sent = call(functools.partial(spread_kernel, shards), S((shards, LANES), f32), (queries,), [VMEM], 1 << 16)
-    ends, keys, values = call(
+    sent = call(
+        functools.partial(spread_kernel, shards),
+        S((shards, LANES), f32),
+        (queries,),
+        [VMEM],
+        1 << 16,
+    )
+    live, ends, keys, values = call(
         prepare_kernel,
-        (S((pairs, pages, 2 * dim), bf16), S((pairs, CAP * PAGE, dim), bf16), S((pairs, CAP * PAGE, dim), bf16)),
+        (
+            S((pairs, LANES), f32),
+            S((pairs, pages, 2 * dim), bf16),
+            S((pairs, CAP * PAGE, dim), bf16),
+            S((pairs, CAP * PAGE, dim), bf16),
+        ),
         (shard_counts, page_list, key_cache, value_cache),
-        [SMEM, SMEM, VMEM, VMEM],
+        [HBM, HBM, HBM, HBM],
         1 << 23,
+        [
+            pltpu.VMEM(shard_counts.shape, jnp.int32),
+            pltpu.SMEM(page_list.shape, jnp.int32),
+            pltpu.VMEM((pairs, tokens, dim), bf16),
+            pltpu.VMEM((pairs, tokens, dim), bf16),
+            pltpu.SemaphoreType.DMA((2,)),
+            pltpu.SemaphoreType.DMA((pairs,)),
+            pltpu.SemaphoreType.DMA((pairs,)),
+        ],
+        53,
     )
     gathered = exchanged(sent, "seq")
     weight = jnp.transpose(out_weight.reshape(width, devices, width), (1, 0, 2)).reshape(devices, width * width)
     parts, bound = call(
         scores_kernel,
         (S((2 * shards, LANES), f32), S((batch, heads, pages), f32)),
-        (shard_counts, gathered, ends, keys, values),
-        [SMEM, VMEM, VMEM, VMEM, VMEM],
+        (live, gathered, ends, keys, values),
+        [VMEM, VMEM, VMEM, VMEM, VMEM],
         1 << 20,
     )
     arrived = exchanged(parts, "seq")

time: 67 us -> 62.6 us (0.934)
  starting transfers between devices: 28.8 us -> 25.1 us
  local copies, waits for them, and re-layouts: 7.88 us -> 4.69 us
  waiting for transfers between devices: 21.5 us -> 24.2 us
    all_to_all x3, starting transfers between devices: 28.8 us -> 25.1 us  [exchanged(): return lax.all_to_all(sent, axis, 0, 0, tiled=True).reshape(x.shape)]
    unnamed x14 -> x8, local copies, waits for them, and re-layouts: 5.24 us -> 2.05 us
    all_to_all x3, waiting for transfers between devices: 21.5 us -> 24.2 us  [exchanged(): return lax.all_to_all(sent, axis, 0, 0, tiled=True).reshape(x.shape)]
  transfers between devices with their start and end apart: 3 -> 3, of which waited for: 3 -> 3; matrix products, arithmetic and copies ran while one was open for 4% -> 4% of each run, Pallas kernels for 5% -> 6%
where the time goes in v2:
time: 62.6 us; the launch traced here: 62.3 us
  starting transfers between devices  25.1 us (40%)
  waiting for transfers between devices  24.2 us (39%)
  Pallas kernels  7.63 us (12%)
  local copies, waits for them, and re-layouts  4.69 us (7%)
  between operations  0.71 us (1%)
    all_to_all x3, starting transfers between devices, exchanged(): return lax.all_to_all(sent, axis, 0, 0, tiled=True).reshape(x.shape)  25.1 us
    all_to_all x3, waiting for transfers between devices, exchanged(): return lax.all_to_all(sent, axis, 0, 0, tiled=True).reshape(x.shape)  24.2 us
    pallas_call x6, Pallas kernels, call(): pl.pallas_call(kernel, out_shape=out_shape, in_specs=specs, out_specs=tup...  7.63 us
    unnamed x8, local copies, waits for them, and re-layouts  2.05 us
    reshape x1, local copies, waits for them, and re-layouts, local(): out_weight.reshape(width, devices, width)  1.64 us
  transfers between devices with their start and end apart: 3, of which 3 were waited for; matrix products, arithmetic and copies ran while one was open for 4% of the time, Pallas kernels for 6%

profile of v2, /device:TPU:1, one launch (start us, length us, event | category | flops | bytes accessed | tf_op | source)
XLA Modules:
  0.0 62.3 jit_solution(13953794446759629415)
XLA Ops:
  0.6 0.0 copy-start.2
  0.6 0.7 %copy-done.2 = bf16[4,32]{1,0:T(4,128)(2,1)S(1)} copy-done((bf16[4,32]{1,0:T(4,128)(2,1)S(1)}, bf16[4,32]{1,0:T(4,128)(2,1)}, u32[]{:S(2)}) %copy-start.2) | copy-done | bytes 280
  1.3 0.7 %shard_map.86 = f32[64,128]{1,0:T(8,128)} custom-call(bf16[4,32]{1,0:T(4,128)(2,1)S(1)} %copy-done.2), custom_call_target="tpu_custom_call" | custom-call | bytes 65536 | tf_op jit(solution)/shard_map/pallas_call | solution.py:211
  2.0 13.0 %all-to-all-start = ((f32[64,1,128]{2,1,0:T(1,128)}), f32[64,1,128]{2,1,0:T(1,128)S(1)}, u32[]{:S(2)}, u32[]{:S(2)}) async-start(f32[64,1,128]{2,1,0:T(1,128)} %bitcast.1), calls=%async_computation | async-start | bytes 65536 | tf_op jit(solution)/shard_map/all_to_all | solution.py:225
  15.0 0.0 copy-start
  15.0 0.7 %copy-done = s32[4,2,256]{2,1,0:T(2,128)S(1)} copy-done((s32[4,2,256]{2,1,0:T(2,128)S(1)}, s32[4,2,256]{2,1,0:T(2,128)}, u32[]{:S(2)}) %copy-start) | copy-done | bytes 8216
  15.7 0.0 copy-start.1
  15.7 0.7 %copy-done.1 = s32[4,2,64]{2,1,0:T(2,128)S(1)} copy-done((s32[4,2,64]{2,1,0:T(2,128)S(1)}, s32[4,2,64]{2,1,0:T(2,128)}, u32[]{:S(2)}) %copy-start.1) | copy-done | bytes 2072
  16.4 0.0 copy-start.3
  16.4 2.9 %shard_map.85 = (f32[8,128]{1,0:T(8,128)S(1)}, bf16[8,64,256]{2,1,0:T(8,128)(2,1)S(1)}, bf16[8,128,128]{2,1,0:T(8,128)(2,1)S(1)}, bf16[8,128,128]{2,1,0:T(8,128)(2,1)S(1)}) custom-call(s32[4,2,64]{2,1,0:T(2,128)S(1)} %copy-done.1, s32[4,2,256]{2,1,0:T(2,128)S(1)} %copy-done, bf16[4,2,1024,128]{3,2,1,0:T(8,128)(2,1)} %key_hbm.1, ...), custom_call_target="tpu_custom_call" | custom-call | bytes 8388608 | tf_op jit(solution)/shard_map/pallas_call | solution.py:211
  19.2 5.0 %all-to-all-done = f32[64,1,128]{2,1,0:T(1,128)S(1)} async-done(((f32[64,1,128]{2,1,0:T(1,128)}), f32[64,1,128]{2,1,0:T(1,128)S(1)}, u32[]{:S(2)}, u32[]{:S(2)}) %all-to-all-start) | async-done | bytes 32800 | tf_op jit(solution)/shard_map/all_to_all | solution.py:225
  24.2 1.4 %shard_map.87 = (f32[128,128]{1,0:T(8,128)}, f32[4,16,64]{2,1,0:T(8,128)S(1)}) custom-call(f32[8,128]{1,0:T(8,128)S(1)} %get-tuple-element.11.live_ref, f32[64,128]{1,0:T(8,128)S(1)} %bitcast.15, bf16[8,64,256]{2,1,0:T(8,128)(2,1)S(1)} %get-tuple-element.12.ends_ref, bf16[8,128,128]{2,1,0:T(8,128)(2,1)S(1)} %get-tuple-element.13.keys_ref, ...), custom_call_target="tpu_custom_call" | custom-call | bytes 1048576 | tf_op jit(solution)/shard_map/pallas_call | solution.py:211
  25.6 5.4 %all-to-all-start.1 = ((f32[64,2,128]{2,1,0:T(2,128)}), f32[64,2,128]{2,1,0:T(2,128)S(1)}, u32[]{:S(2)}, u32[]{:S(2)}) async-start(f32[64,2,128]{2,1,0:T(2,128)} %bitcast.3), calls=%async_computation.1 | async-start | bytes 131072 | tf_op jit(solution)/shard_map/all_to_all | solution.py:225
  31.0 0.0 copy-done.3
  31.0 1.6 %reshape.34 = bf16[32,256,32]{2,1,0:T(8,128)(2,1)S(1)} reshape(bf16[32,8192]{1,0:T(8,128)(2,1)S(1)} %copy-done.3) | data formatting | bytes 1048576 | tf_op jit(solution)/shard_map/reshape | solution.py:269
  32.7 0.8 %copy.13 = bf16[256,32,32]{0,2,1:T(8,128)(2,1)S(1)} copy(bf16[256,32,32]{2,0,1:T(8,128)(2,1)S(1)} %bitcast.16) | data formatting | bytes 1048576 | tf_op jit(solution)/shard_map/transpose | solution.py:269
  33.5 0.2 copy.14.weight_ref
  33.7 7.1 %all-to-all-done.1 = f32[64,2,128]{2,1,0:T(2,128)S(1)} async-done(((f32[64,2,128]{2,1,0:T(2,128)}), f32[64,2,128]{2,1,0:T(2,128)S(1)}, u32[]{:S(2)}, u32[]{:S(2)}) %all-to-all-start.1) | async-done | bytes 65568 | tf_op jit(solution)/shard_map/all_to_all | solution.py:225
  40.8 1.2 %shard_map.88 = (bf16[4,32]{1,0:T(4,128)(2,1)}, f32[256,128]{1,0:T(8,128)}) custom-call(f32[128,128]{1,0:T(8,128)S(1)} %bitcast.12, bf16[256,1024]{1,0:T(8,128)(2,1)S(1)} %copy.14.weight_ref), custom_call_target="tpu_custom_call" | custom-call | bytes 1048576 | tf_op jit(solution)/shard_map/pallas_call | solution.py:211
  42.0 6.7 %all-to-all-start.2 = ((f32[256,1,128]{2,1,0:T(1,128)}), f32[256,1,128]{2,1,0:T(1,128)S(1)}, u32[]{:S(2)}, u32[]{:S(2)}) async-start(f32[256,1,128]{2,1,0:T(1,128)} %bitcast.8), calls=%async_computation.2 | async-start | bytes 262144 | tf_op jit(solution)/shard_map/all_to_all | solution.py:225
  48.8 0.7 %shard_map.90 = f32[4,16,64]{2,1,0:T(8,128)} custom-call(f32[128,128]{1,0:T(8,128)S(1)} %bitcast.13, f32[4,16,64]{2,1,0:T(8,128)S(1)} %get-tuple-element.18.bound_ref), custom_call_target="tpu_custom_call" | custom-call | bytes 262144 | tf_op jit(solution)/shard_map/pallas_call | solution.py:211
  49.5 12.1 %all-to-all-done.2 = f32[256,1,128]{2,1,0:T(1,128)S(1)} async-done(((f32[256,1,128]{2,1,0:T(1,128)}), f32[256,1,128]{2,1,0:T(1,128)S(1)}, u32[]{:S(2)}, u32[]{:S(2)}) %all-to-all-start.2) | async-done | bytes 131104 | tf_op jit(solution)/shard_map/all_to_all | solution.py:225
  61.6 0.7 %shard_map.89 = bf16[4,32]{1,0:T(4,128)(2,1)} custom-call(f32[256,128]{1,0:T(8,128)S(1)} %bitcast.14), custom_call_target="tpu_custom_call" | custom-call | bytes 131072 | tf_op jit(solution)/shard_map/pallas_call | solution.py:211
Async XLA Ops:
  0.6 0.7 %copy-start.2 = (bf16[4,32]{1,0:T(4,128)(2,1)S(1)}, bf16[4,32]{1,0:T(4,128)(2,1)}, u32[]{:S(2)}) copy-start(bf16[4,32]{1,0:T(4,128)(2,1)} %query_ref.1) | copy-start | bytes 772
  2.0 22.2 %all-to-all-start = ((f32[64,1,128]{2,1,0:T(1,128)}), f32[64,1,128]{2,1,0:T(1,128)S(1)}, u32[]{:S(2)}, u32[]{:S(2)}) async-start(f32[64,1,128]{2,1,0:T(1,128)} %bitcast.1), calls=%async_computation | async-start | bytes 65536 | tf_op jit(solution)/shard_map/all_to_all | solution.py:225
  15.0 0.7 %copy-start = (s32[4,2,256]{2,1,0:T(2,128)S(1)}, s32[4,2,256]{2,1,0:T(2,128)}, u32[]{:S(2)}) copy-start(s32[4,2,256]{2,1,0:T(2,128)} %pages_hbm.1) | copy-start | bytes 24580
  15.7 0.7 %copy-start.1 = (s32[4,2,64]{2,1,0:T(2,128)S(1)}, s32[4,2,64]{2,1,0:T(2,128)}, u32[]{:S(2)}) copy-start(s32[4,2,64]{2,1,0:T(2,128)} %counts_hbm.1) | copy-start | bytes 6148
  16.4 14.7 %copy-start.3 = (bf16[32,8192]{1,0:T(8,128)(2,1)S(1)}, bf16[32,8192]{1,0:T(8,128)(2,1)}, u32[]{:S(2)}) copy-start(bf16[32,8192]{1,0:T(8,128)(2,1)} %param.11) | copy-start | bytes 1572868
  25.6 15.2 %all-to-all-start.1 = ((f32[64,2,128]{2,1,0:T(2,128)}), f32[64,2,128]{2,1,0:T(2,128)S(1)}, u32[]{:S(2)}, u32[]{:S(2)}) async-start(f32[64,2,128]{2,1,0:T(2,128)} %bitcast.3), calls=%async_computation.1 | async-start | bytes 131072 | tf_op jit(solution)/shard_map/all_to_all | solution.py:225
  42.0 19.6 %all-to-all-start.2 = ((f32[256,1,128]{2,1,0:T(1,128)}), f32[256,1,128]{2,1,0:T(1,128)S(1)}, u32[]{:S(2)}, u32[]{:S(2)}) async-start(f32[256,1,128]{2,1,0:T(1,128)} %bitcast.8), calls=%async_computation.2 | async-start | bytes 262144 | tf_op jit(solution)/shard_map/all_to_all | solution.py:225

commit v3 on v2

--- a/solution.py
+++ b/solution.py
@@ -147,44 +147,61 @@
         part_ref[pl.ds(2 * q + 1, heads, stride=8), :] = seconds
 
 
-def project_kernel(part_ref, weight_ref, attention_ref, out_ref):
+def merged_line(part_ref):
     shards = part_ref.shape[0] // 2
-    width = LANES // 4
     values = part_ref[pl.ds(0, shards, stride=2), :]
     logs = part_ref[pl.ds(1, shards, stride=2), :]
     shares = jnp.exp(logs - jnp.max(logs, axis=0, keepdims=True))
-    block = block_lanes((shards, LANES), width)
+    block = block_lanes((shards, LANES), LANES // 4)
     spread = jnp.zeros((shards, LANES), jnp.float32)
     for b in range(4):
         at = LANES // 2 + b
         spread = jnp.where(block == b, shares[:, at : at + 1], spread)
     line = jnp.sum(spread * values, axis=0, keepdims=True) / jnp.sum(spread, axis=0, keepdims=True)
-    for b in range(4):
-        attention_ref[b : b + 1, :] = line[:, b * width : (b + 1) * width].astype(jnp.bfloat16)
-    line = line.astype(jnp.bfloat16).astype(jnp.float32)
-    lanes = lax.broadcasted_iota(jnp.int32, (width, LANES), 1)
-    subs = lax.broadcasted_iota(jnp.int32, (width, LANES), 0)
-    picked = jnp.where(lanes % width == subs, line, 0.0).astype(jnp.bfloat16)
-    same = (
-        lax.broadcasted_iota(jnp.int32, (LANES, LANES), 0) // width
-        == block_lanes((LANES, LANES), width)
-    )
-    turned = jnp.dot(
-        picked, jnp.where(same, 1.0, 0.0).astype(jnp.bfloat16), preferred_element_type=jnp.float32
-    )
-    diagonal = lanes % width == subs
-    wide = jnp.concatenate(
-        [jnp.where(diagonal, turned[k : k + 1, :], 0.0).astype(jnp.bfloat16) for k in range(width)],
-        axis=0,
-    )
-    out_ref[...] = jnp.dot(weight_ref[...], wide, preferred_element_type=jnp.float32)
-
-
-def mass_kernel(part_ref, bound_ref, mass_ref):
+    return line.astype(jnp.bfloat16)
+
+
+def project_kernel(part_ref, weight_ref, out_ref):
+    width = LANES // 4
+    columns = weight_ref.shape[1]
+    chunk = 4 * LANES
+    line = merged_line(part_ref).astype(jnp.float32)
+    rows = [line[:, b * width : (b + 1) * width] for b in range(4)]
+    small = lax.broadcasted_iota(jnp.int32, (8, width), 0)
+    sides = []
+    for d in range(4):
+        side = jnp.zeros((8, width), jnp.float32)
+        for b in range(4):
+            side = jnp.where((small + d) % 4 == b, rows[b], side)
+        sides.append(side)
+    left = jnp.concatenate(sides, axis=0).astype(jnp.bfloat16)
+    subs = lax.broadcasted_iota(jnp.int32, (8, LANES), 0)
+    block = block_lanes((8, LANES), width)
+    for start in range(0, columns, chunk):
+        terms = jnp.dot(left, weight_ref[:, start : start + chunk], preferred_element_type=jnp.float32)
+        for pair in range(0, chunk, 2 * LANES):
+            found = jnp.zeros((8, LANES), jnp.float32)
+            for d in range(4):
+                turn = terms[8 * d : 8 * (d + 1), pair : pair + 2 * LANES]
+                turn = jnp.where(subs < 4, turn[:, :LANES], turn[:, LANES:])
+                turn = pltpu.roll(turn, d * width, 1) if d else turn
+                found = jnp.where(block == (subs + d) % 4, turn, found)
+            at = (start + pair) // width
+            out_ref[at : at + 8, :] = found
+
+
+def finish_kernel(terms_ref, part_ref, bound_ref, output_ref, attention_ref, mass_ref):
     batch, heads, pages = bound_ref.shape
     shards = part_ref.shape[0] // 2
     group = HQ // KVH
     groups = heads // group
+    width = LANES // 4
+    sums = jnp.sum(terms_ref[...], axis=0, keepdims=True)
+    attention = merged_line(part_ref)
+    for b in range(batch):
+        columns = slice(b * width, (b + 1) * width)
+        output_ref[b : b + 1, :] = sums[:, columns].astype(jnp.bfloat16)
+        attention_ref[b : b + 1, :] = attention[:, columns]
     logs = part_ref[pl.ds(1, shards, stride=2), :]
     peak = jnp.max(logs, axis=0, keepdims=True)
     line = peak + jnp.log(jnp.sum(jnp.exp(logs - peak), axis=0, keepdims=True))
@@ -198,12 +215,6 @@
             )
             rows = slice(g * group, (g + 1) * group)
             mass_ref[b, rows, :] = jnp.exp(bound_ref[b, rows, :] - column)
-
-
-def total_kernel(width, terms_ref, out_ref):
-    line = jnp.sum(terms_ref[...], axis=0, keepdims=True)
-    for b in range(out_ref.shape[0]):
-        out_ref[b : b + 1, :] = line[:, b * width : (b + 1) * width].astype(out_ref.dtype)
 
 
 def call(kernel, out_shape, args, specs, nbytes, scratch=(), limit=32):
@@ -266,7 +277,6 @@
         53,
     )
     gathered = exchanged(sent, "seq")
-    weight = jnp.transpose(out_weight.reshape(width, devices, width), (1, 0, 2)).reshape(devices, width * width)
     parts, bound = call(
         scores_kernel,
         (S((2 * shards, LANES), f32), S((batch, heads, pages), f32)),
@@ -275,17 +285,15 @@
         1 << 20,
     )
     arrived = exchanged(parts, "seq")
-    attention, terms = call(
-        project_kernel,
-        (S((batch, width), bf16), S((devices, LANES), f32)),
-        (arrived, weight),
-        [VMEM, VMEM],
-        1 << 20,
-    )
-    page_mass = call(mass_kernel, S((batch, heads, pages), f32), (arrived, bound), [VMEM, VMEM], 1 << 18)
+    terms = call(project_kernel, S((devices, LANES), f32), (arrived, out_weight), [VMEM, VMEM], 1 << 20)
     landed = exchanged(terms, ("head", "seq"))
-    output = call(functools.partial(total_kernel, width), S((batch, width), bf16), (landed,), [VMEM], 1 << 17)
-    return (output, attention, page_mass)
+    return call(
+        finish_kernel,
+        (S((batch, width), bf16), S((batch, width), bf16), S((batch, heads, pages), f32)),
+        (landed, arrived, bound),
+        [VMEM, VMEM, VMEM],
+        1 << 18,
+    )
 
 
 def solution(mesh):

time: 62.6 us -> 61.3 us (0.979)
  blocking collectives: 0 us -> 34.4 us
  waiting for transfers between devices: 24.2 us -> 4.96 us
  starting transfers between devices: 25.1 us -> 13 us
  local copies, waits for them, and re-layouts: 4.69 us -> 2.05 us
  Pallas kernels: 7.63 us -> 5.97 us
    all_to_all x0 -> x2, blocking collectives: none -> 34.4 us  [exchanged(): return lax.all_to_all(sent, axis, 0, 0, tiled=True).reshape(x.shape)]
    all_to_all x3 -> x1, waiting for transfers between devices: 24.2 us -> 4.96 us  [exchanged(): return lax.all_to_all(sent, axis, 0, 0, tiled=True).reshape(x.shape)]
    all_to_all x3 -> x1, starting transfers between devices: 25.1 us -> 13 us  [exchanged(): return lax.all_to_all(sent, axis, 0, 0, tiled=True).reshape(x.shape)]
    reshape x2 -> x0, local copies, waits for them, and re-layouts: 1.84 us -> none  [the longest x1 1.64 us: local(): out_weight.reshape(width, devices, width)]
    pallas_call x6 -> x5, Pallas kernels: 7.63 us -> 5.97 us  [call(): pl.pallas_call(kernel, out_shape=out_shape, in_specs=specs, out_specs=tup...]
    transpose x1 -> x0, local copies, waits for them, and re-layouts: 0.8 us -> none  [local(): jnp.transpose(out_weight.reshape(width, devices, width), (1, 0, 2))]
  transfers between devices with their start and end apart: 3 -> 1, of which waited for: 3 -> 1; matrix products, arithmetic and copies ran while one was open for 4% -> 0% of each run, Pallas kernels for 6% -> 5%
where the time goes in v3:
time: 61.3 us; the launch traced here: 61 us
  blocking collectives  34.4 us (56%)
  starting transfers between devices  13 us (21%)
  Pallas kernels  5.97 us (10%)
  waiting for transfers between devices  4.96 us (8%)
  local copies, waits for them, and re-layouts  2.05 us (3%)
  between operations  0.68 us (1%)
    all_to_all x2, blocking collectives, exchanged(): return lax.all_to_all(sent, axis, 0, 0, tiled=True).reshape(x.shape)  34.4 us
    all_to_all x1, starting transfers between devices, exchanged(): return lax.all_to_all(sent, axis, 0, 0, tiled=True).reshape(x.shape)  13 us
    pallas_call x5, Pallas kernels, call(): pl.pallas_call(kernel, out_shape=out_shape, in_specs=specs, out_specs=tup...  5.97 us
    all_to_all x1, waiting for transfers between devices, exchanged(): return lax.all_to_all(sent, axis, 0, 0, tiled=True).reshape(x.shape)  4.96 us
    unnamed x8, local copies, waits for them, and re-layouts  2.05 us
  transfers between devices with their start and end apart: 1, of which 1 were waited for; matrix products, arithmetic and copies ran while one was open for 0% of the time, Pallas kernels for 5%

profile of v3, /device:TPU:1, one launch (start us, length us, event | category | flops | bytes accessed | tf_op | source)
XLA Modules:
  0.0 61.0 jit_solution(8102909415600878556)
XLA Ops:
  0.6 0.0 copy-start.3
  0.6 0.7 %copy-done.3 = bf16[4,32]{1,0:T(4,128)(2,1)S(1)} copy-done((bf16[4,32]{1,0:T(4,128)(2,1)S(1)}, bf16[4,32]{1,0:T(4,128)(2,1)}, u32[]{:S(2)}) %copy-start.3) | copy-done | bytes 280
  1.3 0.7 %shard_map.86 = f32[64,128]{1,0:T(8,128)} custom-call(bf16[4,32]{1,0:T(4,128)(2,1)S(1)} %copy-done.3), custom_call_target="tpu_custom_call" | custom-call | bytes 65536 | tf_op jit(solution)/shard_map/pallas_call | solution.py:222
  2.0 13.0 %all-to-all-start = ((f32[64,1,128]{2,1,0:T(1,128)}), f32[64,1,128]{2,1,0:T(1,128)S(1)}, u32[]{:S(2)}, u32[]{:S(2)}) async-start(f32[64,1,128]{2,1,0:T(1,128)} %bitcast.1), calls=%async_computation | async-start | bytes 65536 | tf_op jit(solution)/shard_map/all_to_all | solution.py:236
  15.0 0.0 copy-start.1
  15.0 0.7 %copy-done.1 = s32[4,2,256]{2,1,0:T(2,128)S(1)} copy-done((s32[4,2,256]{2,1,0:T(2,128)S(1)}, s32[4,2,256]{2,1,0:T(2,128)}, u32[]{:S(2)}) %copy-start.1) | copy-done | bytes 8216
  15.7 0.0 copy-start.2
  15.7 0.7 %copy-done.2 = s32[4,2,64]{2,1,0:T(2,128)S(1)} copy-done((s32[4,2,64]{2,1,0:T(2,128)S(1)}, s32[4,2,64]{2,1,0:T(2,128)}, u32[]{:S(2)}) %copy-start.2) | copy-done | bytes 2072
  16.4 0.0 copy-start
  16.4 2.9 %shard_map.85 = (f32[8,128]{1,0:T(8,128)S(1)}, bf16[8,64,256]{2,1,0:T(8,128)(2,1)S(1)}, bf16[8,128,128]{2,1,0:T(8,128)(2,1)S(1)}, bf16[8,128,128]{2,1,0:T(8,128)(2,1)S(1)}) custom-call(s32[4,2,64]{2,1,0:T(2,128)S(1)} %copy-done.2, s32[4,2,256]{2,1,0:T(2,128)S(1)} %copy-done.1, bf16[4,2,1024,128]{3,2,1,0:T(8,128)(2,1)} %key_hbm.1, ...), custom_call_target="tpu_custom_call" | custom-call | bytes 8388608 | tf_op jit(solution)/shard_map/pallas_call | solution.py:222
  19.2 5.0 %all-to-all-done = f32[64,1,128]{2,1,0:T(1,128)S(1)} async-done(((f32[64,1,128]{2,1,0:T(1,128)}), f32[64,1,128]{2,1,0:T(1,128)S(1)}, u32[]{:S(2)}, u32[]{:S(2)}) %all-to-all-start) | async-done | bytes 32800 | tf_op jit(solution)/shard_map/all_to_all | solution.py:236
  24.2 0.8 %shard_map.87 = (f32[128,128]{1,0:T(8,128)S(1)}, f32[4,16,64]{2,1,0:T(8,128)S(1)}) custom-call(f32[8,128]{1,0:T(8,128)S(1)} %get-tuple-element.9.live_ref, f32[64,128]{1,0:T(8,128)S(1)} %bitcast.14, bf16[8,64,256]{2,1,0:T(8,128)(2,1)S(1)} %get-tuple-element.10.ends_ref, bf16[8,128,128]{2,1,0:T(8,128)(2,1)S(1)} %get-tuple-element.11.keys_ref, ...), custom_call_target="tpu_custom_call" | custom-call | bytes 1048576 | tf_op jit(solution)/shard_map/pallas_call | solution.py:222
  25.0 15.0 %all_to_all.15 = f32[64,2,128]{2,1,0:T(2,128)S(1)} all-to-all(f32[64,2,128]{2,1,0:T(2,128)S(1)} %bitcast.15), channel_id=1, replica_groups=mesh['head'=4,'seq'=64] {'seq'}, dimensions={0} | all-to-all | bytes 131072 | tf_op jit(solution)/shard_map/all_to_all | solution.py:236
  40.0 0.0 copy-done
  40.0 0.8 %shard_map.88 = f32[256,128]{1,0:T(8,128)S(1)} custom-call(f32[128,128]{1,0:T(8,128)S(1)} %bitcast.10, bf16[32,8192]{1,0:T(8,128)(2,1)S(1)} %copy-done), custom_call_target="tpu_custom_call" | custom-call | bytes 1048576 | tf_op jit(solution)/shard_map/pallas_call | solution.py:222
  40.8 19.4 %all_to_all.16 = f32[256,1,128]{2,1,0:T(1,128)S(1)} all-to-all(f32[256,1,128]{2,1,0:T(1,128)S(1)} %bitcast.13), channel_id=1, replica_groups=mesh['head'=4,'seq'=64] {'head','seq'}, dimensions={0} | all-to-all | bytes 262144 | tf_op jit(solution)/shard_map/all_to_all | solution.py:236
  60.2 0.9 %shard_map.89 = (bf16[4,32]{1,0:T(4,128)(2,1)}, bf16[4,32]{1,0:T(4,128)(2,1)}, f32[4,16,64]{2,1,0:T(8,128)}) custom-call(f32[256,128]{1,0:T(8,128)S(1)} %bitcast.12, f32[128,128]{1,0:T(8,128)S(1)} %bitcast.11, f32[4,16,64]{2,1,0:T(8,128)S(1)} %get-tuple-element.14.bound_ref), custom_call_target="tpu_custom_call" | custom-call | bytes 262144 | tf_op jit(solution)/shard_map/pallas_call | solution.py:222
Async XLA Ops:
  0.6 0.7 %copy-start.3 = (bf16[4,32]{1,0:T(4,128)(2,1)S(1)}, bf16[4,32]{1,0:T(4,128)(2,1)}, u32[]{:S(2)}) copy-start(bf16[4,32]{1,0:T(4,128)(2,1)} %query_ref.1) | copy-start | bytes 772
  2.0 22.2 %all-to-all-start = ((f32[64,1,128]{2,1,0:T(1,128)}), f32[64,1,128]{2,1,0:T(1,128)S(1)}, u32[]{:S(2)}, u32[]{:S(2)}) async-start(f32[64,1,128]{2,1,0:T(1,128)} %bitcast.1), calls=%async_computation | async-start | bytes 65536 | tf_op jit(solution)/shard_map/all_to_all | solution.py:236
  15.0 0.7 %copy-start.1 = (s32[4,2,256]{2,1,0:T(2,128)S(1)}, s32[4,2,256]{2,1,0:T(2,128)}, u32[]{:S(2)}) copy-start(s32[4,2,256]{2,1,0:T(2,128)} %pages_hbm.1) | copy-start | bytes 24580
  15.7 0.7 %copy-start.2 = (s32[4,2,64]{2,1,0:T(2,128)S(1)}, s32[4,2,64]{2,1,0:T(2,128)}, u32[]{:S(2)}) copy-start(s32[4,2,64]{2,1,0:T(2,128)} %counts_hbm.1) | copy-start | bytes 6148
  16.4 23.6 %copy-start = (bf16[32,8192]{1,0:T(8,128)(2,1)S(1)}, bf16[32,8192]{1,0:T(8,128)(2,1)}, u32[]{:S(2)}) copy-start(bf16[32,8192]{1,0:T(8,128)(2,1)} %weight_ref.1) | copy-start | bytes 1572868

commit v4 on v3

--- a/solution.py
+++ b/solution.py
@@ -13,6 +13,7 @@
 HD = 128
 PAGE = 16
 CAP = 8
+SELECT = 256
 LANES = 128
 NEGATIVE = -1e30
 SCALE = 1.0 / math.sqrt(HD)
@@ -32,17 +33,17 @@
 
 
 def prepare_kernel(
-    counts_hbm, pages_hbm, key_hbm, value_hbm,
+    lists_hbm, key_hbm, value_hbm,
     live_ref, ends_ref, keys_out, values_out,
-    counts_ref, pages_ref, key_ref, value_ref, list_sems, key_sems, value_sems,
+    lists_ref, pages_ref, offset_ref, spot_ref, wide_ref, key_ref, value_ref, list_sems, key_sems, value_sems,
 ):
     batch, groups, tokens, dim = key_hbm.shape
     pages = tokens // PAGE
     shard = lax.axis_index("seq")
     pairs = [(b, g) for b in range(batch) for g in range(groups)]
     lists = [
-        pltpu.make_async_copy(counts_hbm, counts_ref, list_sems.at[0]),
-        pltpu.make_async_copy(pages_hbm, pages_ref, list_sems.at[1]),
+        pltpu.make_async_copy(lists_hbm, lists_ref, list_sems.at[0]),
+        pltpu.make_async_copy(lists_hbm, pages_ref, list_sems.at[1]),
     ]
     key_copies = [
         pltpu.make_async_copy(key_hbm.at[b, g], key_ref.at[n], key_sems.at[n])
@@ -54,33 +55,40 @@
     ]
     for copy in lists + key_copies + value_copies:
         copy.start()
-    for copy in lists:
-        copy.wait()
-    chosen = []
+    lists[0].wait()
     for n, (b, g) in enumerate(pairs):
-        counts = counts_ref[b, g : g + 1, :]
-        slots = lax.broadcasted_iota(jnp.int32, counts.shape, 1)
-        offset = jnp.sum(jnp.where(slots < shard, counts, 0))
-        count = jnp.sum(jnp.where(slots == shard, counts, 0), axis=1, keepdims=True)
+        line = lists_ref[b, g : g + 1, :]
+        index = lax.broadcasted_iota(jnp.int32, line.shape, 1) - SELECT
+        earlier = jnp.where((index >= 0) & (index < shard), line, 0)
+        count = jnp.sum(jnp.where(index == shard, line, 0), axis=1, keepdims=True)
         lanes = lax.broadcasted_iota(jnp.int32, (1, LANES), 1)
         live_ref[n : n + 1, :] = jnp.where(lanes // PAGE < count, 1.0, 0.0)
-        starts = []
-        for slot in range(CAP):
-            at = jnp.minimum(offset + slot, pages_ref.shape[2] - 1)
-            page = jnp.clip(pages_ref[b, g, at] - shard * pages, 0, pages - 1)
-            starts.append(pl.multiple_of(page * PAGE, PAGE))
-        chosen.append(starts)
+        offset = jnp.sum(earlier, axis=1, keepdims=True)
+        offset_ref[n : n + 1, :] = jnp.broadcast_to(offset, (1, LANES))
+    offsets = pltpu.make_async_copy(offset_ref, spot_ref, list_sems.at[2])
+    offsets.start()
     for n in range(len(pairs)):
         key_copies[n].wait()
-        paged = key_ref[n].reshape(pages, PAGE, dim)
-        ends_ref[n, :, :dim] = jnp.max(paged, axis=1)
-        ends_ref[n, :, dim:] = jnp.min(paged, axis=1)
-        for slot in range(CAP):
-            keys_out[n, slot * PAGE : (slot + 1) * PAGE, :] = key_ref[n, pl.ds(chosen[n][slot], PAGE), :]
-    for n in range(len(pairs)):
+        wide_ref[...] = key_ref[n].astype(jnp.float32)
+        largest = wide_ref[pl.ds(0, pages, stride=PAGE), :]
+        smallest = largest
+        for row in range(1, PAGE):
+            other = wide_ref[pl.ds(row, pages, stride=PAGE), :]
+            largest = jnp.maximum(largest, other)
+            smallest = jnp.minimum(smallest, other)
+        ends_ref[n, :, :dim] = largest.astype(jnp.bfloat16)
+        ends_ref[n, :, dim:] = smallest.astype(jnp.bfloat16)
+    lists[1].wait()
+    offsets.wait()
+    for n, (b, g) in enumerate(pairs):
         value_copies[n].wait()
         for slot in range(CAP):
-            values_out[n, slot * PAGE : (slot + 1) * PAGE, :] = value_ref[n, pl.ds(chosen[n][slot], PAGE), :]
+            at = jnp.minimum(spot_ref[n, 0] + slot, SELECT - 1)
+            page = jnp.clip(pages_ref[b, g, at] - shard * pages, 0, pages - 1)
+            start = pl.multiple_of(page * PAGE, PAGE)
+            rows = slice(slot * PAGE, (slot + 1) * PAGE)
+            keys_out[n, rows, :] = key_ref[n, pl.ds(start, PAGE), :]
+            values_out[n, rows, :] = value_ref[n, pl.ds(start, PAGE), :]
 
 
 def scores_kernel(live_ref, query_ref, ends_ref, keys_ref, values_ref, part_ref, bound_ref):
@@ -254,6 +262,8 @@
         [VMEM],
         1 << 16,
     )
+    sent, page_list, shard_counts = lax.optimization_barrier((sent, page_list, shard_counts))
+    lists = jnp.concatenate([page_list, shard_counts], axis=2)
     live, ends, keys, values = call(
         prepare_kernel,
         (
@@ -262,15 +272,18 @@
             S((pairs, CAP * PAGE, dim), bf16),
             S((pairs, CAP * PAGE, dim), bf16),
         ),
-        (shard_counts, page_list, key_cache, value_cache),
-        [HBM, HBM, HBM, HBM],
+        (lists, key_cache, value_cache),
+        [HBM, HBM, HBM],
         1 << 23,
         [
-            pltpu.VMEM(shard_counts.shape, jnp.int32),
-            pltpu.SMEM(page_list.shape, jnp.int32),
+            pltpu.VMEM(lists.shape, jnp.int32),
+            pltpu.SMEM(lists.shape, jnp.int32),
+            pltpu.VMEM((pairs, LANES), jnp.int32),
+            pltpu.SMEM((pairs, LANES), jnp.int32),
+            pltpu.VMEM((tokens, dim), f32),
             pltpu.VMEM((pairs, tokens, dim), bf16),
             pltpu.VMEM((pairs, tokens, dim), bf16),
-            pltpu.SemaphoreType.DMA((2,)),
+            pltpu.SemaphoreType.DMA((3,)),
             pltpu.SemaphoreType.DMA((pairs,)),
             pltpu.SemaphoreType.DMA((pairs,)),
         ],

time: 61.3 us -> 60.8 us (level)
  local copies, waits for them, and re-layouts: 2.05 us -> 0.68 us
  other arithmetic: 0 us -> 0.72 us
    unnamed x8 -> x4, local copies, waits for them, and re-layouts: 2.05 us -> 0.68 us
    concatenate x0 -> x1, other arithmetic: none -> 0.72 us  [local(): lists = jnp.concatenate([page_list, shard_counts], axis=2)]
  transfers between devices with their start and end apart: 1 -> 1, of which waited for: 1 -> 1; matrix products, arithmetic and copies ran while one was open for 0% -> 1% of each run, Pallas kernels for 5% -> 5%
where the time goes in v4:
time: 60.8 us; the launch traced here: 60.5 us
  blocking collectives  33.9 us (56%)
  starting transfers between devices  13 us (21%)
  Pallas kernels  6.11 us (10%)
  waiting for transfers between devices  5.49 us (9%)
  other arithmetic  0.72 us (1%)
  local copies, waits for them, and re-layouts  0.68 us (1%)
  between operations  0.67 us (1%)
    all_to_all x2, blocking collectives, exchanged(): return lax.all_to_all(sent, axis, 0, 0, tiled=True).reshape(x.shape)  33.9 us
    all_to_all x1, starting transfers between devices, exchanged(): return lax.all_to_all(sent, axis, 0, 0, tiled=True).reshape(x.shape)  13 us
    pallas_call x5, Pallas kernels, call(): pl.pallas_call(kernel, out_shape=out_shape, in_specs=specs, out_specs=tup...  6.11 us
    all_to_all x1, waiting for transfers between devices, exchanged(): return lax.all_to_all(sent, axis, 0, 0, tiled=True).reshape(x.shape)  5.49 us
  transfers between devices with their start and end apart: 1, of which 1 were waited for; matrix products, arithmetic and copies ran while one was open for 1% of the time, Pallas kernels for 5%

profile of v4, /device:TPU:1, one launch (start us, length us, event | category | flops | bytes accessed | tf_op | source)
XLA Modules:
  0.0 60.5 jit_solution(9616978286716446672)
XLA Ops:
  0.6 0.0 copy-start.1
  0.6 0.7 %copy-done.1 = bf16[4,32]{1,0:T(4,128)(2,1)S(1)} copy-done((bf16[4,32]{1,0:T(4,128)(2,1)S(1)}, bf16[4,32]{1,0:T(4,128)(2,1)}, u32[]{:S(2)}) %copy-start.1) | copy-done | bytes 280
  1.3 0.7 %shard_map.85 = f32[64,128]{1,0:T(8,128)} custom-call(bf16[4,32]{1,0:T(4,128)(2,1)S(1)} %copy-done.1), custom_call_target="tpu_custom_call" | custom-call | bytes 65536 | tf_op jit(solution)/shard_map/pallas_call | solution.py:230
  2.0 13.0 %all-to-all-start = ((f32[64,1,128]{2,1,0:T(1,128)}), f32[64,1,128]{2,1,0:T(1,128)S(1)}, u32[]{:S(2)}, u32[]{:S(2)}) async-start(f32[64,1,128]{2,1,0:T(1,128)} %bitcast.1), calls=%async_computation | async-start | bytes 65536 | tf_op jit(solution)/shard_map/all_to_all | solution.py:244
  15.0 0.7 %pad_add_fusion.lists_hbm = s32[4,2,320]{2,1,0:T(2,128)S(1)} fusion(s32[4,2,64]{2,1,0:T(2,128)} %param.10, s32[4,2,256]{2,1,0:T(2,128)} %param.9), kind=kLoop, calls=%fused_computation | loop fusion | flops 2560 | bytes 20480 | tf_op jit(solution)/shard_map/concatenate | solution.py:266
  15.7 0.0 copy-start
  15.7 3.0 %shard_map.86 = (f32[8,128]{1,0:T(8,128)S(1)}, bf16[8,64,256]{2,1,0:T(8,128)(2,1)S(1)}, bf16[8,128,128]{2,1,0:T(8,128)(2,1)S(1)}, bf16[8,128,128]{2,1,0:T(8,128)(2,1)S(1)}) custom-call(s32[4,2,320]{2,1,0:T(2,128)S(1)} %pad_add_fusion.lists_hbm, bf16[4,2,1024,128]{3,2,1,0:T(8,128)(2,1)} %key_hbm.1, bf16[4,2,1024,128]{3,2,1,0:T(8,128)(2,1)} %value_hbm.1), custom_call_target="tpu_custom_call" | custom-call | bytes 8388608 | tf_op jit(solution)/shard_map/pallas_call | solution.py:230
  18.7 5.5 %all-to-all-done = f32[64,1,128]{2,1,0:T(1,128)S(1)} async-done(((f32[64,1,128]{2,1,0:T(1,128)}), f32[64,1,128]{2,1,0:T(1,128)S(1)}, u32[]{:S(2)}, u32[]{:S(2)}) %all-to-all-start) | async-done | bytes 32800 | tf_op jit(solution)/shard_map/all_to_all | solution.py:244
  24.2 0.8 %shard_map.87 = (f32[128,128]{1,0:T(8,128)S(1)}, f32[4,16,64]{2,1,0:T(8,128)S(1)}) custom-call(f32[8,128]{1,0:T(8,128)S(1)} %get-tuple-element.14.live_ref, f32[64,128]{1,0:T(8,128)S(1)} %bitcast.14, bf16[8,64,256]{2,1,0:T(8,128)(2,1)S(1)} %get-tuple-element.16.ends_ref, bf16[8,128,128]{2,1,0:T(8,128)(2,1)S(1)} %get-tuple-element.17.keys_ref, ...), custom_call_target="tpu_custom_call" | custom-call | bytes 1048576 | tf_op jit(solution)/shard_map/pallas_call | solution.py:230
  25.0 14.4 %all_to_all.15 = f32[64,2,128]{2,1,0:T(2,128)S(1)} all-to-all(f32[64,2,128]{2,1,0:T(2,128)S(1)} %bitcast.15), channel_id=1, replica_groups=mesh['head'=4,'seq'=64] {'seq'}, dimensions={0} | all-to-all | bytes 131072 | tf_op jit(solution)/shard_map/all_to_all | solution.py:244
  39.5 0.0 copy-done
  39.5 0.8 %shard_map.88 = f32[256,128]{1,0:T(8,128)S(1)} custom-call(f32[128,128]{1,0:T(8,128)S(1)} %bitcast.10, bf16[32,8192]{1,0:T(8,128)(2,1)S(1)} %copy-done), custom_call_target="tpu_custom_call" | custom-call | bytes 1048576 | tf_op jit(solution)/shard_map/pallas_call | solution.py:230
  40.2 19.4 %all_to_all.16 = f32[256,1,128]{2,1,0:T(1,128)S(1)} all-to-all(f32[256,1,128]{2,1,0:T(1,128)S(1)} %bitcast.13), channel_id=1, replica_groups=mesh['head'=4,'seq'=64] {'head','seq'}, dimensions={0} | all-to-all | bytes 262144 | tf_op jit(solution)/shard_map/all_to_all | solution.py:244
  59.6 0.9 %shard_map.89 = (bf16[4,32]{1,0:T(4,128)(2,1)}, bf16[4,32]{1,0:T(4,128)(2,1)}, f32[4,16,64]{2,1,0:T(8,128)}) custom-call(f32[256,128]{1,0:T(8,128)S(1)} %bitcast.12, f32[128,128]{1,0:T(8,128)S(1)} %bitcast.11, f32[4,16,64]{2,1,0:T(8,128)S(1)} %get-tuple-element.20.bound_ref), custom_call_target="tpu_custom_call" | custom-call | bytes 262144 | tf_op jit(solution)/shard_map/pallas_call | solution.py:230
Async XLA Ops:
  0.6 0.7 %copy-start.1 = (bf16[4,32]{1,0:T(4,128)(2,1)S(1)}, bf16[4,32]{1,0:T(4,128)(2,1)}, u32[]{:S(2)}) copy-start(bf16[4,32]{1,0:T(4,128)(2,1)} %query_ref.1) | copy-start | bytes 772
  2.0 22.2 %all-to-all-start = ((f32[64,1,128]{2,1,0:T(1,128)}), f32[64,1,128]{2,1,0:T(1,128)S(1)}, u32[]{:S(2)}, u32[]{:S(2)}) async-start(f32[64,1,128]{2,1,0:T(1,128)} %bitcast.1), calls=%async_computation | async-start | bytes 65536 | tf_op jit(solution)/shard_map/all_to_all | solution.py:244
  15.7 23.7 %copy-start = (bf16[32,8192]{1,0:T(8,128)(2,1)S(1)}, bf16[32,8192]{1,0:T(8,128)(2,1)}, u32[]{:S(2)}) copy-start(bf16[32,8192]{1,0:T(8,128)(2,1)} %weight_ref.1) | copy-start | bytes 1572868

commit v5 on v4

--- a/solution.py
+++ b/solution.py
@@ -33,40 +33,35 @@
 
 
 def prepare_kernel(
-    lists_hbm, key_hbm, value_hbm,
-    live_ref, ends_ref, keys_out, values_out,
-    lists_ref, pages_ref, offset_ref, spot_ref, wide_ref, key_ref, value_ref, list_sems, key_sems, value_sems,
+    lists_ref, key_hbm,
+    live_ref, start_ref, ends_ref, keys_out,
+    spot_ref, wide_ref, key_ref, spot_sem, key_sems,
 ):
     batch, groups, tokens, dim = key_hbm.shape
     pages = tokens // PAGE
     shard = lax.axis_index("seq")
     pairs = [(b, g) for b in range(batch) for g in range(groups)]
-    lists = [
-        pltpu.make_async_copy(lists_hbm, lists_ref, list_sems.at[0]),
-        pltpu.make_async_copy(lists_hbm, pages_ref, list_sems.at[1]),
-    ]
     key_copies = [
         pltpu.make_async_copy(key_hbm.at[b, g], key_ref.at[n], key_sems.at[n])
         for n, (b, g) in enumerate(pairs)
     ]
-    value_copies = [
-        pltpu.make_async_copy(value_hbm.at[b, g], value_ref.at[n], value_sems.at[n])
-        for n, (b, g) in enumerate(pairs)
-    ]
-    for copy in lists + key_copies + value_copies:
+    for copy in key_copies:
         copy.start()
-    lists[0].wait()
-    for n, (b, g) in enumerate(pairs):
-        line = lists_ref[b, g : g + 1, :]
-        index = lax.broadcasted_iota(jnp.int32, line.shape, 1) - SELECT
-        earlier = jnp.where((index >= 0) & (index < shard), line, 0)
-        count = jnp.sum(jnp.where(index == shard, line, 0), axis=1, keepdims=True)
-        lanes = lax.broadcasted_iota(jnp.int32, (1, LANES), 1)
-        live_ref[n : n + 1, :] = jnp.where(lanes // PAGE < count, 1.0, 0.0)
-        offset = jnp.sum(earlier, axis=1, keepdims=True)
-        offset_ref[n : n + 1, :] = jnp.broadcast_to(offset, (1, LANES))
-    offsets = pltpu.make_async_copy(offset_ref, spot_ref, list_sems.at[2])
-    offsets.start()
+    lists = jnp.concatenate([lists_ref[b] for b in range(batch)], axis=0)
+    listed, counts = lists[:, :SELECT], lists[:, SELECT:]
+    index = lax.broadcasted_iota(jnp.int32, counts.shape, 1)
+    offset = jnp.sum(jnp.where(index < shard, counts, 0), axis=1, keepdims=True)
+    count = jnp.sum(jnp.where(index == shard, counts, 0), axis=1, keepdims=True)
+    lanes = lax.broadcasted_iota(jnp.int32, (len(pairs), LANES), 1)
+    live_ref[...] = jnp.where(lanes // PAGE < count, 1.0, 0.0)
+    place = lax.broadcasted_iota(jnp.int32, listed.shape, 1)
+    page = jnp.zeros((len(pairs), LANES), jnp.int32)
+    for slot in range(CAP):
+        found = jnp.sum(jnp.where(place == offset + slot, listed, 0), axis=1, keepdims=True)
+        page = jnp.where(lanes == slot, found, page)
+    start_ref[...] = jnp.clip(page - shard * pages, 0, pages - 1) * PAGE
+    spots = pltpu.make_async_copy(start_ref, spot_ref, spot_sem)
+    spots.start()
     for n in range(len(pairs)):
         key_copies[n].wait()
         wide_ref[...] = key_ref[n].astype(jnp.float32)
@@ -78,20 +73,23 @@
             smallest = jnp.minimum(smallest, other)
         ends_ref[n, :, :dim] = largest.astype(jnp.bfloat16)
         ends_ref[n, :, dim:] = smallest.astype(jnp.bfloat16)
-    lists[1].wait()
-    offsets.wait()
-    for n, (b, g) in enumerate(pairs):
-        value_copies[n].wait()
+    spots.wait()
+    starts = [
+        [pl.multiple_of(spot_ref[n, slot], PAGE) for slot in range(CAP)] for n in range(len(pairs))
+    ]
+    for n in range(len(pairs)):
         for slot in range(CAP):
-            at = jnp.minimum(spot_ref[n, 0] + slot, SELECT - 1)
-            page = jnp.clip(pages_ref[b, g, at] - shard * pages, 0, pages - 1)
-            start = pl.multiple_of(page * PAGE, PAGE)
             rows = slice(slot * PAGE, (slot + 1) * PAGE)
-            keys_out[n, rows, :] = key_ref[n, pl.ds(start, PAGE), :]
-            values_out[n, rows, :] = value_ref[n, pl.ds(start, PAGE), :]
-
-
-def scores_kernel(live_ref, query_ref, ends_ref, keys_ref, values_ref, part_ref, bound_ref):
+            keys_out[n, rows, :] = key_ref[n, pl.ds(starts[n][slot], PAGE), :]
+
+
+def scores_kernel(
+    live_ref, start_ref, query_ref, ends_ref, keys_ref, value_ref,
+    part_ref, bound_ref,
+    spot_ref, spot_sem,
+):
+    spots = pltpu.make_async_copy(start_ref, spot_ref, spot_sem)
+    spots.start()
     batch, heads, _ = bound_ref.shape
     groups = live_ref.shape[0] // batch
     group = heads // groups
@@ -111,11 +109,10 @@
     subs = lax.broadcasted_iota(jnp.int32, (group, LANES), 0)
     page_row = jnp.zeros((group, LANES), jnp.float32)
     head_rows = [jnp.zeros((group, LANES), jnp.float32) for _ in range(groups)]
-    mixed = []
+    shares = []
     contract = (((1,), (1,)), ((), ()))
     for b in range(batch):
         rows = rows_of(b)
-        parts = []
         for g in range(groups):
             n = b * groups + g
             query = rows[g * group : (g + 1) * group]
@@ -135,13 +132,25 @@
             top = jnp.max(scores, axis=1, keepdims=True)
             weights = jnp.where(live, jnp.exp(scores - top), 0.0)
             total = jnp.maximum(jnp.sum(weights, axis=1, keepdims=True), 1e-30)
-            unnormed = jnp.dot(
-                weights.astype(jnp.bfloat16), values_ref[n], preferred_element_type=jnp.float32
-            )
-            parts.append(unnormed / total)
+            shares.append((weights.astype(jnp.bfloat16), total))
             head_rows[g] = jnp.where(
                 lanes == LANES // 2 + b, top + jnp.log(total), head_rows[g]
             )
+    spots.wait()
+    mixed = []
+    for b in range(batch):
+        parts = []
+        for g in range(groups):
+            n = b * groups + g
+            weights, total = shares[n]
+            values = jnp.concatenate(
+                [
+                    value_ref[b, g, pl.ds(pl.multiple_of(spot_ref[n, slot], PAGE), PAGE), :]
+                    for slot in range(CAP)
+                ],
+                axis=0,
+            )
+            parts.append(jnp.dot(weights, values, preferred_element_type=jnp.float32) / total)
         mixed.append(jnp.concatenate(parts, axis=0))
     page_line = jnp.sum(page_row, axis=0, keepdims=True)
     seconds = jnp.concatenate(head_rows, axis=0) + page_line
@@ -264,38 +273,34 @@
     )
     sent, page_list, shard_counts = lax.optimization_barrier((sent, page_list, shard_counts))
     lists = jnp.concatenate([page_list, shard_counts], axis=2)
-    live, ends, keys, values = call(
+    live, starts, ends, keys = call(
         prepare_kernel,
         (
             S((pairs, LANES), f32),
+            S((pairs, LANES), jnp.int32),
             S((pairs, pages, 2 * dim), bf16),
             S((pairs, CAP * PAGE, dim), bf16),
-            S((pairs, CAP * PAGE, dim), bf16),
         ),
-        (lists, key_cache, value_cache),
-        [HBM, HBM, HBM],
-        1 << 23,
+        (lists, key_cache),
+        [VMEM, HBM],
+        1 << 22,
         [
-            pltpu.VMEM(lists.shape, jnp.int32),
-            pltpu.SMEM(lists.shape, jnp.int32),
-            pltpu.VMEM((pairs, LANES), jnp.int32),
             pltpu.SMEM((pairs, LANES), jnp.int32),
             pltpu.VMEM((tokens, dim), f32),
             pltpu.VMEM((pairs, tokens, dim), bf16),
-            pltpu.VMEM((pairs, tokens, dim), bf16),
-            pltpu.SemaphoreType.DMA((3,)),
-            pltpu.SemaphoreType.DMA((pairs,)),
+            pltpu.SemaphoreType.DMA,
             pltpu.SemaphoreType.DMA((pairs,)),
         ],
-        53,
+        52,
     )
     gathered = exchanged(sent, "seq")
     parts, bound = call(
         scores_kernel,
         (S((2 * shards, LANES), f32), S((batch, heads, pages), f32)),
-        (live, gathered, ends, keys, values),
-        [VMEM, VMEM, VMEM, VMEM, VMEM],
+        (live, starts, gathered, ends, keys, value_cache),
+        [VMEM, VMEM, VMEM, VMEM, VMEM, VMEM],
         1 << 20,
+        [pltpu.SMEM((pairs, LANES), jnp.int32), pltpu.SemaphoreType.DMA],
     )
     arrived = exchanged(parts, "seq")
     terms = call(project_kernel, S((devices, LANES), f32), (arrived, out_weight), [VMEM, VMEM], 1 << 20)

time: 60.8 us -> 60.6 us (level)
  transfers between devices with their start and end apart: 1 -> 1, of which waited for: 1 -> 1; matrix products, arithmetic and copies ran while one was open for 1% -> 1% of each run, Pallas kernels for 5% -> 4%
where the time goes in v5:
time: 60.6 us; the launch traced here: 60.3 us
  blocking collectives  33.4 us (55%)
  starting transfers between devices  13 us (21%)
  waiting for transfers between devices  5.92 us (10%)
  Pallas kernels  5.76 us (10%)
  local copies, waits for them, and re-layouts  0.83 us (1%)
  other arithmetic  0.72 us (1%)
  between operations  0.68 us (1%)
    all_to_all x2, blocking collectives, exchanged(): return lax.all_to_all(sent, axis, 0, 0, tiled=True).reshape(x.shape)  33.4 us
    all_to_all x1, starting transfers between devices, exchanged(): return lax.all_to_all(sent, axis, 0, 0, tiled=True).reshape(x.shape)  13 us
    all_to_all x1, waiting for transfers between devices, exchanged(): return lax.all_to_all(sent, axis, 0, 0, tiled=True).reshape(x.shape)  5.92 us
    pallas_call x5, Pallas kernels, call(): pl.pallas_call(kernel, out_shape=out_shape, in_specs=specs, out_specs=tup...  5.76 us
  transfers between devices with their start and end apart: 1, of which 1 were waited for; matrix products, arithmetic and copies ran while one was open for 1% of the time, Pallas kernels for 4%

profile of v5, /device:TPU:1, one launch (start us, length us, event | category | flops | bytes accessed | tf_op | source)
XLA Modules:
  0.0 60.3 jit_solution(6712225012130830248)
XLA Ops:
  0.6 0.0 copy-start
  0.6 0.0 copy-start.2
  0.6 0.8 %copy-done.2 = bf16[4,32]{1,0:T(4,128)(2,1)S(1)} copy-done((bf16[4,32]{1,0:T(4,128)(2,1)S(1)}, bf16[4,32]{1,0:T(4,128)(2,1)}, u32[]{:S(2)}) %copy-start.2) | copy-done | bytes 280
  1.5 0.7 %shard_map.85 = f32[64,128]{1,0:T(8,128)} custom-call(bf16[4,32]{1,0:T(4,128)(2,1)S(1)} %copy-done.2), custom_call_target="tpu_custom_call" | custom-call | bytes 65536 | tf_op jit(solution)/shard_map/pallas_call | solution.py:239
  2.2 13.0 %all-to-all-start = ((f32[64,1,128]{2,1,0:T(1,128)}), f32[64,1,128]{2,1,0:T(1,128)S(1)}, u32[]{:S(2)}, u32[]{:S(2)}) async-start(f32[64,1,128]{2,1,0:T(1,128)} %bitcast.1), calls=%async_computation | async-start | bytes 65536 | tf_op jit(solution)/shard_map/all_to_all | solution.py:253
  15.2 0.7 %pad_add_fusion.lists_ref = s32[4,2,320]{2,1,0:T(2,128)S(1)} fusion(s32[4,2,64]{2,1,0:T(2,128)} %param.10, s32[4,2,256]{2,1,0:T(2,128)} %param.9), kind=kLoop, calls=%fused_computation | loop fusion | flops 2560 | bytes 20480 | tf_op jit(solution)/shard_map/concatenate | solution.py:275
  15.9 0.0 copy-start.1
  15.9 2.6 %shard_map.86 = (f32[8,128]{1,0:T(8,128)S(1)}, s32[8,128]{1,0:T(8,128)S(1)}, bf16[8,64,256]{2,1,0:T(8,128)(2,1)S(1)}, bf16[8,128,128]{2,1,0:T(8,128)(2,1)S(1)}) custom-call(s32[4,2,320]{2,1,0:T(2,128)S(1)} %pad_add_fusion.lists_ref, bf16[4,2,1024,128]{3,2,1,0:T(8,128)(2,1)} %key_hbm.1), custom_call_target="tpu_custom_call" | custom-call | bytes 4194304 | tf_op jit(solution)/shard_map/pallas_call | solution.py:239
  18.4 5.9 %all-to-all-done = f32[64,1,128]{2,1,0:T(1,128)S(1)} async-done(((f32[64,1,128]{2,1,0:T(1,128)}), f32[64,1,128]{2,1,0:T(1,128)S(1)}, u32[]{:S(2)}, u32[]{:S(2)}) %all-to-all-start) | async-done | bytes 32800 | tf_op jit(solution)/shard_map/all_to_all | solution.py:253
  24.4 0.0 copy-done
  24.4 0.9 %shard_map.87 = (f32[128,128]{1,0:T(8,128)S(1)}, f32[4,16,64]{2,1,0:T(8,128)S(1)}) custom-call(f32[8,128]{1,0:T(8,128)S(1)} %get-tuple-element.14.live_ref, s32[8,128]{1,0:T(8,128)S(1)} %get-tuple-element.15.start_ref, f32[64,128]{1,0:T(8,128)S(1)} %bitcast.14, bf16[8,64,256]{2,1,0:T(8,128)(2,1)S(1)} %get-tuple-element.17.ends_ref, ...), custom_call_target="tpu_custom_call" | custom-call | bytes 1048576 | tf_op jit(solution)/shard_map/pallas_call | solution.py:239
  25.3 14.0 %all_to_all.15 = f32[64,2,128]{2,1,0:T(2,128)S(1)} all-to-all(f32[64,2,128]{2,1,0:T(2,128)S(1)} %bitcast.15), channel_id=1, replica_groups=mesh['head'=4,'seq'=64] {'seq'}, dimensions={0} | all-to-all | bytes 131072 | tf_op jit(solution)/shard_map/all_to_all | solution.py:253
  39.3 0.0 copy-done.1
  39.3 0.8 %shard_map.88 = f32[256,128]{1,0:T(8,128)S(1)} custom-call(f32[128,128]{1,0:T(8,128)S(1)} %bitcast.10, bf16[32,8192]{1,0:T(8,128)(2,1)S(1)} %copy-done.1), custom_call_target="tpu_custom_call" | custom-call | bytes 1048576 | tf_op jit(solution)/shard_map/pallas_call | solution.py:239
  40.1 19.4 %all_to_all.16 = f32[256,1,128]{2,1,0:T(1,128)S(1)} all-to-all(f32[256,1,128]{2,1,0:T(1,128)S(1)} %bitcast.13), channel_id=1, replica_groups=mesh['head'=4,'seq'=64] {'head','seq'}, dimensions={0} | all-to-all | bytes 262144 | tf_op jit(solution)/shard_map/all_to_all | solution.py:253
  59.5 0.9 %shard_map.89 = (bf16[4,32]{1,0:T(4,128)(2,1)}, bf16[4,32]{1,0:T(4,128)(2,1)}, f32[4,16,64]{2,1,0:T(8,128)}) custom-call(f32[256,128]{1,0:T(8,128)S(1)} %bitcast.12, f32[128,128]{1,0:T(8,128)S(1)} %bitcast.11, f32[4,16,64]{2,1,0:T(8,128)S(1)} %get-tuple-element.20.bound_ref), custom_call_target="tpu_custom_call" | custom-call | bytes 262144 | tf_op jit(solution)/shard_map/pallas_call | solution.py:239
Async XLA Ops:
  0.6 23.7 %copy-start = (bf16[4,2,1024,128]{3,2,1,0:T(8,128)(2,1)S(1)}, bf16[4,2,1024,128]{3,2,1,0:T(8,128)(2,1)}, u32[]{:S(2)}) copy-start(bf16[4,2,1024,128]{3,2,1,0:T(8,128)(2,1)} %value_ref.1) | copy-start | bytes 6291460
  0.6 0.8 %copy-start.2 = (bf16[4,32]{1,0:T(4,128)(2,1)S(1)}, bf16[4,32]{1,0:T(4,128)(2,1)}, u32[]{:S(2)}) copy-start(bf16[4,32]{1,0:T(4,128)(2,1)} %query_ref.1) | copy-start | bytes 772
  2.2 22.2 %all-to-all-start = ((f32[64,1,128]{2,1,0:T(1,128)}), f32[64,1,128]{2,1,0:T(1,128)S(1)}, u32[]{:S(2)}, u32[]{:S(2)}) async-start(f32[64,1,128]{2,1,0:T(1,128)} %bitcast.1), calls=%async_computation | async-start | bytes 65536 | tf_op jit(solution)/shard_map/all_to_all | solution.py:253
  15.9 23.4 %copy-start.1 = (bf16[32,8192]{1,0:T(8,128)(2,1)S(1)}, bf16[32,8192]{1,0:T(8,128)(2,1)}, u32[]{:S(2)}) copy-start(bf16[32,8192]{1,0:T(8,128)(2,1)} %weight_ref.1) | copy-start | bytes 1572868

commit v6 on v5

--- a/solution.py
+++ b/solution.py
@@ -32,10 +32,29 @@
     out_ref[...] = jnp.broadcast_to(line, (copies, LANES))
 
 
+def folded_rows(pieces, combine):
+    rows = lax.broadcasted_iota(jnp.int32, pieces[0].shape, 0)
+
+    def step(first, second, keep, shift):
+        kept = jnp.where(keep, first, second)
+        other = jnp.where(keep, second, first)
+        return combine(kept, pltpu.roll(other, shift, 0))
+
+    def four(a, b, c, d, turn):
+        at = (rows + turn) % 8
+        left = step(a, b, at < 4, 4)
+        right = step(c, d, (at < 2) | (at >= 6), 4)
+        return step(left, right, at % 4 >= 2, 2)
+
+    odd = four(pieces[3], pieces[7], pieces[1], pieces[5], 0)
+    even = four(pieces[2], pieces[6], pieces[0], pieces[4], 1)
+    return step(odd, even, rows % 2 == 1, 1)
+
+
 def prepare_kernel(
     lists_ref, key_hbm,
     live_ref, start_ref, ends_ref, keys_out,
-    spot_ref, wide_ref, key_ref, spot_sem, key_sems,
+    spot_ref, key_ref, spot_sem, key_sems,
 ):
     batch, groups, tokens, dim = key_hbm.shape
     pages = tokens // PAGE
@@ -47,32 +66,35 @@
     ]
     for copy in key_copies:
         copy.start()
-    lists = jnp.concatenate([lists_ref[b] for b in range(batch)], axis=0)
+    lists = jnp.concatenate([lists_ref[b] for b in range(batch)], axis=0).astype(jnp.float32)
     listed, counts = lists[:, :SELECT], lists[:, SELECT:]
     index = lax.broadcasted_iota(jnp.int32, counts.shape, 1)
-    offset = jnp.sum(jnp.where(index < shard, counts, 0), axis=1, keepdims=True)
-    count = jnp.sum(jnp.where(index == shard, counts, 0), axis=1, keepdims=True)
+    offset = jnp.sum(jnp.where(index < shard, counts, 0.0), axis=1, keepdims=True).astype(jnp.int32)
+    count = jnp.sum(jnp.where(index == shard, counts, 0.0), axis=1, keepdims=True).astype(jnp.int32)
     lanes = lax.broadcasted_iota(jnp.int32, (len(pairs), LANES), 1)
     live_ref[...] = jnp.where(lanes // PAGE < count, 1.0, 0.0)
     place = lax.broadcasted_iota(jnp.int32, listed.shape, 1)
-    page = jnp.zeros((len(pairs), LANES), jnp.int32)
+    page = jnp.zeros((len(pairs), LANES), jnp.float32)
     for slot in range(CAP):
-        found = jnp.sum(jnp.where(place == offset + slot, listed, 0), axis=1, keepdims=True)
+        found = jnp.sum(jnp.where(place == offset + slot, listed, 0.0), axis=1, keepdims=True)
         page = jnp.where(lanes == slot, found, page)
-    start_ref[...] = jnp.clip(page - shard * pages, 0, pages - 1) * PAGE
+    start_ref[...] = jnp.clip(page.astype(jnp.int32) - shard * pages, 0, pages - 1) * PAGE
     spots = pltpu.make_async_copy(start_ref, spot_ref, spot_sem)
     spots.start()
     for n in range(len(pairs)):
         key_copies[n].wait()
-        wide_ref[...] = key_ref[n].astype(jnp.float32)
-        largest = wide_ref[pl.ds(0, pages, stride=PAGE), :]
-        smallest = largest
-        for row in range(1, PAGE):
-            other = wide_ref[pl.ds(row, pages, stride=PAGE), :]
-            largest = jnp.maximum(largest, other)
-            smallest = jnp.minimum(smallest, other)
-        ends_ref[n, :, :dim] = largest.astype(jnp.bfloat16)
-        ends_ref[n, :, dim:] = smallest.astype(jnp.bfloat16)
+        for first in range(0, pages, 16):
+            largest, smallest = [], []
+            for half in (first, first + 8):
+                wide = key_ref[n, half * PAGE : (half + 8) * PAGE, :].astype(jnp.float32)
+                parts = [wide[8 * k : 8 * (k + 1)] for k in range(PAGE)]
+                above = [jnp.maximum(parts[2 * k], parts[2 * k + 1]) for k in range(8)]
+                below = [jnp.minimum(parts[2 * k], parts[2 * k + 1]) for k in range(8)]
+                largest.append(folded_rows(above, jnp.maximum))
+                smallest.append(folded_rows(below, jnp.minimum))
+            at = slice(first, first + 16)
+            ends_ref[n, at, :dim] = jnp.concatenate(largest, axis=0).astype(jnp.bfloat16)
+            ends_ref[n, at, dim:] = jnp.concatenate(smallest, axis=0).astype(jnp.bfloat16)
     spots.wait()
     starts = [
         [pl.multiple_of(spot_ref[n, slot], PAGE) for slot in range(CAP)] for n in range(len(pairs))
@@ -286,7 +308,6 @@
         1 << 22,
         [
             pltpu.SMEM((pairs, LANES), jnp.int32),
-            pltpu.VMEM((tokens, dim), f32),
             pltpu.VMEM((pairs, tokens, dim), bf16),
             pltpu.SemaphoreType.DMA,
             pltpu.SemaphoreType.DMA((pairs,)),

time: 60.6 us -> 60.4 us (level)
  transfers between devices with their start and end apart: 1 -> 1, of which waited for: 1 -> 1; matrix products, arithmetic and copies ran while one was open for 1% -> 1% of each run, Pallas kernels for 4% -> 3%
where the time goes in v6:
time: 60.4 us; the launch traced here: 60.1 us
  blocking collectives  33.2 us (55%)
  starting transfers between devices  13 us (22%)
  waiting for transfers between devices  6.5 us (11%)
  Pallas kernels  5.18 us (9%)
  local copies, waits for them, and re-layouts  0.83 us (1%)
  other arithmetic  0.72 us (1%)
  between operations  0.68 us (1%)
    all_to_all x2, blocking collectives, exchanged(): return lax.all_to_all(sent, axis, 0, 0, tiled=True).reshape(x.shape)  33.2 us
    all_to_all x1, starting transfers between devices, exchanged(): return lax.all_to_all(sent, axis, 0, 0, tiled=True).reshape(x.shape)  13 us
    all_to_all x1, waiting for transfers between devices, exchanged(): return lax.all_to_all(sent, axis, 0, 0, tiled=True).reshape(x.shape)  6.5 us
    pallas_call x5, Pallas kernels, call(): pl.pallas_call(kernel, out_shape=out_shape, in_specs=specs, out_specs=tup...  5.18 us
  transfers between devices with their start and end apart: 1, of which 1 were waited for; matrix products, arithmetic and copies ran while one was open for 1% of the time, Pallas kernels for 3%

profile of v6, /device:TPU:1, one launch (start us, length us, event | category | flops | bytes accessed | tf_op | source)
XLA Modules:
  0.0 60.1 jit_solution(12759327539155367514)
XLA Ops:
  0.6 0.0 copy-start
  0.6 0.0 copy-start.2
  0.6 0.8 %copy-done.2 = bf16[4,32]{1,0:T(4,128)(2,1)S(1)} copy-done((bf16[4,32]{1,0:T(4,128)(2,1)S(1)}, bf16[4,32]{1,0:T(4,128)(2,1)}, u32[]{:S(2)}) %copy-start.2) | copy-done | bytes 280
  1.5 0.7 %shard_map.85 = f32[64,128]{1,0:T(8,128)} custom-call(bf16[4,32]{1,0:T(4,128)(2,1)S(1)} %copy-done.2), custom_call_target="tpu_custom_call" | custom-call | bytes 65536 | tf_op jit(solution)/shard_map/pallas_call | solution.py:261
  2.2 13.0 %all-to-all-start = ((f32[64,1,128]{2,1,0:T(1,128)}), f32[64,1,128]{2,1,0:T(1,128)S(1)}, u32[]{:S(2)}, u32[]{:S(2)}) async-start(f32[64,1,128]{2,1,0:T(1,128)} %bitcast.1), calls=%async_computation | async-start | bytes 65536 | tf_op jit(solution)/shard_map/all_to_all | solution.py:275
  15.2 0.7 %pad_add_fusion.lists_ref = s32[4,2,320]{2,1,0:T(2,128)S(1)} fusion(s32[4,2,64]{2,1,0:T(2,128)} %param.10, s32[4,2,256]{2,1,0:T(2,128)} %param.9), kind=kLoop, calls=%fused_computation | loop fusion | flops 2560 | bytes 20480 | tf_op jit(solution)/shard_map/concatenate | solution.py:297
  15.9 0.0 copy-start.1
  15.9 2.0 %shard_map.86 = (f32[8,128]{1,0:T(8,128)S(1)}, s32[8,128]{1,0:T(8,128)S(1)}, bf16[8,64,256]{2,1,0:T(8,128)(2,1)S(1)}, bf16[8,128,128]{2,1,0:T(8,128)(2,1)S(1)}) custom-call(s32[4,2,320]{2,1,0:T(2,128)S(1)} %pad_add_fusion.lists_ref, bf16[4,2,1024,128]{3,2,1,0:T(8,128)(2,1)} %key_hbm.1), custom_call_target="tpu_custom_call" | custom-call | bytes 4194304 | tf_op jit(solution)/shard_map/pallas_call | solution.py:261
  17.9 6.5 %all-to-all-done = f32[64,1,128]{2,1,0:T(1,128)S(1)} async-done(((f32[64,1,128]{2,1,0:T(1,128)}), f32[64,1,128]{2,1,0:T(1,128)S(1)}, u32[]{:S(2)}, u32[]{:S(2)}) %all-to-all-start) | async-done | bytes 32800 | tf_op jit(solution)/shard_map/all_to_all | solution.py:275
  24.4 0.0 copy-done
  24.4 0.9 %shard_map.87 = (f32[128,128]{1,0:T(8,128)S(1)}, f32[4,16,64]{2,1,0:T(8,128)S(1)}) custom-call(f32[8,128]{1,0:T(8,128)S(1)} %get-tuple-element.14.live_ref, s32[8,128]{1,0:T(8,128)S(1)} %get-tuple-element.15.start_ref, f32[64,128]{1,0:T(8,128)S(1)} %bitcast.14, bf16[8,64,256]{2,1,0:T(8,128)(2,1)S(1)} %get-tuple-element.17.ends_ref, ...), custom_call_target="tpu_custom_call" | custom-call | bytes 1048576 | tf_op jit(solution)/shard_map/pallas_call | solution.py:261
  25.3 13.8 %all_to_all.15 = f32[64,2,128]{2,1,0:T(2,128)S(1)} all-to-all(f32[64,2,128]{2,1,0:T(2,128)S(1)} %bitcast.15), channel_id=1, replica_groups=mesh['head'=4,'seq'=64] {'seq'}, dimensions={0} | all-to-all | bytes 131072 | tf_op jit(solution)/shard_map/all_to_all | solution.py:275
  39.1 0.0 copy-done.1
  39.1 0.8 %shard_map.88 = f32[256,128]{1,0:T(8,128)S(1)} custom-call(f32[128,128]{1,0:T(8,128)S(1)} %bitcast.10, bf16[32,8192]{1,0:T(8,128)(2,1)S(1)} %copy-done.1), custom_call_target="tpu_custom_call" | custom-call | bytes 1048576 | tf_op jit(solution)/shard_map/pallas_call | solution.py:261
  39.8 19.4 %all_to_all.16 = f32[256,1,128]{2,1,0:T(1,128)S(1)} all-to-all(f32[256,1,128]{2,1,0:T(1,128)S(1)} %bitcast.13), channel_id=1, replica_groups=mesh['head'=4,'seq'=64] {'head','seq'}, dimensions={0} | all-to-all | bytes 262144 | tf_op jit(solution)/shard_map/all_to_all | solution.py:275
  59.3 0.9 %shard_map.89 = (bf16[4,32]{1,0:T(4,128)(2,1)}, bf16[4,32]{1,0:T(4,128)(2,1)}, f32[4,16,64]{2,1,0:T(8,128)}) custom-call(f32[256,128]{1,0:T(8,128)S(1)} %bitcast.12, f32[128,128]{1,0:T(8,128)S(1)} %bitcast.11, f32[4,16,64]{2,1,0:T(8,128)S(1)} %get-tuple-element.20.bound_ref), custom_call_target="tpu_custom_call" | custom-call | bytes 262144 | tf_op jit(solution)/shard_map/pallas_call | solution.py:261
Async XLA Ops:
  0.6 23.7 %copy-start = (bf16[4,2,1024,128]{3,2,1,0:T(8,128)(2,1)S(1)}, bf16[4,2,1024,128]{3,2,1,0:T(8,128)(2,1)}, u32[]{:S(2)}) copy-start(bf16[4,2,1024,128]{3,2,1,0:T(8,128)(2,1)} %value_ref.1) | copy-start | bytes 6291460
  0.6 0.8 %copy-start.2 = (bf16[4,32]{1,0:T(4,128)(2,1)S(1)}, bf16[4,32]{1,0:T(4,128)(2,1)}, u32[]{:S(2)}) copy-start(bf16[4,32]{1,0:T(4,128)(2,1)} %query_ref.1) | copy-start | bytes 772
  2.2 22.2 %all-to-all-start = ((f32[64,1,128]{2,1,0:T(1,128)}), f32[64,1,128]{2,1,0:T(1,128)S(1)}, u32[]{:S(2)}, u32[]{:S(2)}) async-start(f32[64,1,128]{2,1,0:T(1,128)} %bitcast.1), calls=%async_computation | async-start | bytes 65536 | tf_op jit(solution)/shard_map/all_to_all | solution.py:275
  15.9 23.2 %copy-start.1 = (bf16[32,8192]{1,0:T(8,128)(2,1)S(1)}, bf16[32,8192]{1,0:T(8,128)(2,1)}, u32[]{:S(2)}) copy-start(bf16[32,8192]{1,0:T(8,128)(2,1)} %weight_ref.1) | copy-start | bytes 1572868

commit v7 on v6

--- a/solution.py
+++ b/solution.py
@@ -186,25 +186,24 @@
         part_ref[pl.ds(2 * q + 1, heads, stride=8), :] = seconds
 
 
-def merged_line(part_ref):
+def project_kernel(part_ref, weight_ref, out_ref, line_ref):
+    width = LANES // 4
+    columns = weight_ref.shape[1]
+    chunk = 4 * LANES
     shards = part_ref.shape[0] // 2
     values = part_ref[pl.ds(0, shards, stride=2), :]
     logs = part_ref[pl.ds(1, shards, stride=2), :]
-    shares = jnp.exp(logs - jnp.max(logs, axis=0, keepdims=True))
-    block = block_lanes((shards, LANES), LANES // 4)
+    peak = jnp.max(logs, axis=0, keepdims=True)
+    shares = jnp.exp(logs - peak)
+    lane_block = block_lanes((shards, LANES), width)
     spread = jnp.zeros((shards, LANES), jnp.float32)
     for b in range(4):
         at = LANES // 2 + b
-        spread = jnp.where(block == b, shares[:, at : at + 1], spread)
+        spread = jnp.where(lane_block == b, shares[:, at : at + 1], spread)
     line = jnp.sum(spread * values, axis=0, keepdims=True) / jnp.sum(spread, axis=0, keepdims=True)
-    return line.astype(jnp.bfloat16)
-
-
-def project_kernel(part_ref, weight_ref, out_ref):
-    width = LANES // 4
-    columns = weight_ref.shape[1]
-    chunk = 4 * LANES
-    line = merged_line(part_ref).astype(jnp.float32)
+    line = line.astype(jnp.bfloat16).astype(jnp.float32)
+    line_ref[0:1, :] = line
+    line_ref[1:2, :] = peak + jnp.log(jnp.sum(shares, axis=0, keepdims=True))
     rows = [line[:, b * width : (b + 1) * width] for b in range(4)]
     small = lax.broadcasted_iota(jnp.int32, (8, width), 0)
     sides = []
@@ -229,21 +228,18 @@
             out_ref[at : at + 8, :] = found
 
 
-def finish_kernel(terms_ref, part_ref, bound_ref, output_ref, attention_ref, mass_ref):
+def finish_kernel(terms_ref, line_ref, bound_ref, output_ref, attention_ref, mass_ref):
     batch, heads, pages = bound_ref.shape
-    shards = part_ref.shape[0] // 2
     group = HQ // KVH
     groups = heads // group
     width = LANES // 4
     sums = jnp.sum(terms_ref[...], axis=0, keepdims=True)
-    attention = merged_line(part_ref)
+    attention = line_ref[0:1, :].astype(jnp.bfloat16)
     for b in range(batch):
         columns = slice(b * width, (b + 1) * width)
         output_ref[b : b + 1, :] = sums[:, columns].astype(jnp.bfloat16)
         attention_ref[b : b + 1, :] = attention[:, columns]
-    logs = part_ref[pl.ds(1, shards, stride=2), :]
-    peak = jnp.max(logs, axis=0, keepdims=True)
-    line = peak + jnp.log(jnp.sum(jnp.exp(logs - peak), axis=0, keepdims=True))
+    line = line_ref[1:2, :]
     lanes = lax.broadcasted_iota(jnp.int32, (group, LANES), 1)
     subs = lax.broadcasted_iota(jnp.int32, (group, LANES), 0)
     for b in range(batch):
@@ -324,12 +320,18 @@
         [pltpu.SMEM((pairs, LANES), jnp.int32), pltpu.SemaphoreType.DMA],
     )
     arrived = exchanged(parts, "seq")
-    terms = call(project_kernel, S((devices, LANES), f32), (arrived, out_weight), [VMEM, VMEM], 1 << 20)
+    terms, line = call(
+        project_kernel,
+        (S((devices, LANES), f32), S((2, LANES), f32)),
+        (arrived, out_weight),
+        [VMEM, VMEM],
+        1 << 20,
+    )
     landed = exchanged(terms, ("head", "seq"))
     return call(
         finish_kernel,
         (S((batch, width), bf16), S((batch, width), bf16), S((batch, heads, pages), f32)),
-        (landed, arrived, bound),
+        (landed, line, bound),
         [VMEM, VMEM, VMEM],
         1 << 18,
     )

time: 60.4 us -> 60.3 us (level)
  no operation moved by 1% of the time
where the time goes in v7:
time: 60.3 us; the launch traced here: 60 us
  blocking collectives  33.2 us (55%)
  starting transfers between devices  13 us (22%)
  waiting for transfers between devices  6.5 us (11%)
  Pallas kernels  5.07 us (8%)
  local copies, waits for them, and re-layouts  0.83 us (1%)
  other arithmetic  0.72 us (1%)
  between operations  0.68 us (1%)
    all_to_all x2, blocking collectives, exchanged(): return lax.all_to_all(sent, axis, 0, 0, tiled=True).reshape(x.shape)  33.2 us
    all_to_all x1, starting transfers between devices, exchanged(): return lax.all_to_all(sent, axis, 0, 0, tiled=True).reshape(x.shape)  13 us
    all_to_all x1, waiting for transfers between devices, exchanged(): return lax.all_to_all(sent, axis, 0, 0, tiled=True).reshape(x.shape)  6.5 us
    pallas_call x5, Pallas kernels, call(): pl.pallas_call(kernel, out_shape=out_shape, in_specs=specs, out_specs=tup...  5.07 us
  transfers between devices with their start and end apart: 1, of which 1 were waited for; matrix products, arithmetic and copies ran while one was open for 1% of the time, Pallas kernels for 3%

profile of v7, /device:TPU:1, one launch (start us, length us, event | category | flops | bytes accessed | tf_op | source)
XLA Modules:
  0.0 60.0 jit_solution(14496550819759158944)
XLA Ops:
  0.6 0.0 copy-start
  0.6 0.0 copy-start.2
  0.6 0.8 %copy-done.2 = bf16[4,32]{1,0:T(4,128)(2,1)S(1)} copy-done((bf16[4,32]{1,0:T(4,128)(2,1)S(1)}, bf16[4,32]{1,0:T(4,128)(2,1)}, u32[]{:S(2)}) %copy-start.2) | copy-done | bytes 280
  1.5 0.7 %shard_map.85 = f32[64,128]{1,0:T(8,128)} custom-call(bf16[4,32]{1,0:T(4,128)(2,1)S(1)} %copy-done.2), custom_call_target="tpu_custom_call" | custom-call | bytes 65536 | tf_op jit(solution)/shard_map/pallas_call | solution.py:257
  2.2 13.0 %all-to-all-start = ((f32[64,1,128]{2,1,0:T(1,128)}), f32[64,1,128]{2,1,0:T(1,128)S(1)}, u32[]{:S(2)}, u32[]{:S(2)}) async-start(f32[64,1,128]{2,1,0:T(1,128)} %bitcast.1), calls=%async_computation | async-start | bytes 65536 | tf_op jit(solution)/shard_map/all_to_all | solution.py:271
  15.2 0.7 %pad_add_fusion.lists_ref = s32[4,2,320]{2,1,0:T(2,128)S(1)} fusion(s32[4,2,64]{2,1,0:T(2,128)} %param.10, s32[4,2,256]{2,1,0:T(2,128)} %param.9), kind=kLoop, calls=%fused_computation | loop fusion | flops 2560 | bytes 20480 | tf_op jit(solution)/shard_map/concatenate | solution.py:293
  15.9 0.0 copy-start.1
  15.9 2.0 %shard_map.86 = (f32[8,128]{1,0:T(8,128)S(1)}, s32[8,128]{1,0:T(8,128)S(1)}, bf16[8,64,256]{2,1,0:T(8,128)(2,1)S(1)}, bf16[8,128,128]{2,1,0:T(8,128)(2,1)S(1)}) custom-call(s32[4,2,320]{2,1,0:T(2,128)S(1)} %pad_add_fusion.lists_ref, bf16[4,2,1024,128]{3,2,1,0:T(8,128)(2,1)} %key_hbm.1), custom_call_target="tpu_custom_call" | custom-call | bytes 4194304 | tf_op jit(solution)/shard_map/pallas_call | solution.py:257
  17.9 6.5 %all-to-all-done = f32[64,1,128]{2,1,0:T(1,128)S(1)} async-done(((f32[64,1,128]{2,1,0:T(1,128)}), f32[64,1,128]{2,1,0:T(1,128)S(1)}, u32[]{:S(2)}, u32[]{:S(2)}) %all-to-all-start) | async-done | bytes 32800 | tf_op jit(solution)/shard_map/all_to_all | solution.py:271
  24.4 0.0 copy-done
  24.4 0.9 %shard_map.87 = (f32[128,128]{1,0:T(8,128)S(1)}, f32[4,16,64]{2,1,0:T(8,128)S(1)}) custom-call(f32[8,128]{1,0:T(8,128)S(1)} %get-tuple-element.16.live_ref, s32[8,128]{1,0:T(8,128)S(1)} %get-tuple-element.17.start_ref, f32[64,128]{1,0:T(8,128)S(1)} %bitcast.13, bf16[8,64,256]{2,1,0:T(8,128)(2,1)S(1)} %get-tuple-element.19.ends_ref, ...), custom_call_target="tpu_custom_call" | custom-call | bytes 1048576 | tf_op jit(solution)/shard_map/pallas_call | solution.py:257
  25.3 13.8 %all_to_all.15 = f32[64,2,128]{2,1,0:T(2,128)S(1)} all-to-all(f32[64,2,128]{2,1,0:T(2,128)S(1)} %bitcast.14), channel_id=1, replica_groups=mesh['head'=4,'seq'=64] {'seq'}, dimensions={0} | all-to-all | bytes 131072 | tf_op jit(solution)/shard_map/all_to_all | solution.py:271
  39.1 0.0 copy-done.1
  39.1 0.8 %shard_map.88 = (f32[256,128]{1,0:T(8,128)S(1)}, f32[2,128]{1,0:T(2,128)S(1)}) custom-call(f32[128,128]{1,0:T(8,128)S(1)} %bitcast.11, bf16[32,8192]{1,0:T(8,128)(2,1)S(1)} %copy-done.1), custom_call_target="tpu_custom_call" | custom-call | bytes 1048576 | tf_op jit(solution)/shard_map/pallas_call | solution.py:257
  39.8 19.4 %all_to_all.16 = f32[256,1,128]{2,1,0:T(1,128)S(1)} all-to-all(f32[256,1,128]{2,1,0:T(1,128)S(1)} %bitcast.12), channel_id=1, replica_groups=mesh['head'=4,'seq'=64] {'head','seq'}, dimensions={0} | all-to-all | bytes 262144 | tf_op jit(solution)/shard_map/all_to_all | solution.py:271
  59.3 0.7 %shard_map.89 = (bf16[4,32]{1,0:T(4,128)(2,1)}, bf16[4,32]{1,0:T(4,128)(2,1)}, f32[4,16,64]{2,1,0:T(8,128)}) custom-call(f32[256,128]{1,0:T(8,128)S(1)} %bitcast.10, f32[2,128]{1,0:T(2,128)S(1)} %get-tuple-element.23.line_ref, f32[4,16,64]{2,1,0:T(8,128)S(1)} %get-tuple-element.24.bound_ref), custom_call_target="tpu_custom_call" | custom-call | bytes 262144 | tf_op jit(solution)/shard_map/pallas_call | solution.py:257
Async XLA Ops:
  0.6 23.7 %copy-start = (bf16[4,2,1024,128]{3,2,1,0:T(8,128)(2,1)S(1)}, bf16[4,2,1024,128]{3,2,1,0:T(8,128)(2,1)}, u32[]{:S(2)}) copy-start(bf16[4,2,1024,128]{3,2,1,0:T(8,128)(2,1)} %value_ref.1) | copy-start | bytes 6291460
  0.6 0.8 %copy-start.2 = (bf16[4,32]{1,0:T(4,128)(2,1)S(1)}, bf16[4,32]{1,0:T(4,128)(2,1)}, u32[]{:S(2)}) copy-start(bf16[4,32]{1,0:T(4,128)(2,1)} %query_ref.1) | copy-start | bytes 772
  2.2 22.2 %all-to-all-start = ((f32[64,1,128]{2,1,0:T(1,128)}), f32[64,1,128]{2,1,0:T(1,128)S(1)}, u32[]{:S(2)}, u32[]{:S(2)}) async-start(f32[64,1,128]{2,1,0:T(1,128)} %bitcast.1), calls=%async_computation | async-start | bytes 65536 | tf_op jit(solution)/shard_map/all_to_all | solution.py:271
  15.9 23.2 %copy-start.1 = (bf16[32,8192]{1,0:T(8,128)(2,1)S(1)}, bf16[32,8192]{1,0:T(8,128)(2,1)}, u32[]{:S(2)}) copy-start(bf16[32,8192]{1,0:T(8,128)(2,1)} %weight_ref.1) | copy-start | bytes 1572868

commit v8 on v7

--- a/solution.py
+++ b/solution.py
@@ -26,7 +26,10 @@
     return lax.broadcasted_iota(jnp.int32, shape, 1) // width
 
 
-def spread_kernel(copies, query_ref, out_ref):
+def spread_kernel(copies, query_hbm, out_ref, query_ref, arrived):
+    copy = pltpu.make_async_copy(query_hbm, query_ref, arrived)
+    copy.start()
+    copy.wait()
     rows = query_ref[...].astype(jnp.float32)
     line = jnp.concatenate([rows[b : b + 1, :] for b in range(rows.shape[0])], axis=1)
     out_ref[...] = jnp.broadcast_to(line, (copies, LANES))
@@ -286,8 +289,10 @@
         functools.partial(spread_kernel, shards),
         S((shards, LANES), f32),
         (queries,),
-        [VMEM],
+        [HBM],
         1 << 16,
+        [pltpu.VMEM(queries.shape, bf16), pltpu.SemaphoreType.DMA],
+        62,
     )
     sent, page_list, shard_counts = lax.optimization_barrier((sent, page_list, shard_counts))
     lists = jnp.concatenate([page_list, shard_counts], axis=2)

time: 60.3 us -> 60.3 us (level)
  local copies, waits for them, and re-layouts: 0.83 us -> 0.01 us
  Pallas kernels: 5.07 us -> 5.75 us
    unnamed x6 -> x4, local copies, waits for them, and re-layouts: 0.83 us -> 0.01 us
    pallas_call x5, Pallas kernels: 5.07 us -> 5.75 us  [call(): pl.pallas_call(kernel, out_shape=out_shape, in_specs=specs, out_specs=tup...]
where the time goes in v8:
time: 60.3 us; the launch traced here: 60 us
  blocking collectives  33.2 us (55%)
  starting transfers between devices  13.1 us (22%)
  waiting for transfers between devices  6.5 us (11%)
  Pallas kernels  5.75 us (10%)
  other arithmetic  0.72 us (1%)
  between operations  0.68 us (1%)
    all_to_all x2, blocking collectives, exchanged(): return lax.all_to_all(sent, axis, 0, 0, tiled=True).reshape(x.shape)  33.2 us
    all_to_all x1, starting transfers between devices, exchanged(): return lax.all_to_all(sent, axis, 0, 0, tiled=True).reshape(x.shape)  13.1 us
    all_to_all x1, waiting for transfers between devices, exchanged(): return lax.all_to_all(sent, axis, 0, 0, tiled=True).reshape(x.shape)  6.5 us
    pallas_call x5, Pallas kernels, call(): pl.pallas_call(kernel, out_shape=out_shape, in_specs=specs, out_specs=tup...  5.75 us
  transfers between devices with their start and end apart: 1, of which 1 were waited for; matrix products, arithmetic and copies ran while one was open for 1% of the time, Pallas kernels for 3%

profile of v8, /device:TPU:1, one launch (start us, length us, event | category | flops | bytes accessed | tf_op | source)
XLA Modules:
  0.0 60.0 jit_solution(746174658853030584)
XLA Ops:
  0.6 1.4 %shard_map.85 = f32[64,128]{1,0:T(8,128)} custom-call(bf16[4,32]{1,0:T(4,128)(2,1)} %query_hbm.1), custom_call_target="tpu_custom_call" | custom-call | bytes 65536 | tf_op jit(solution)/shard_map/pallas_call | solution.py:260
  2.0 0.0 copy-start
  2.0 13.1 %all-to-all-start = ((f32[64,1,128]{2,1,0:T(1,128)}), f32[64,1,128]{2,1,0:T(1,128)S(1)}, u32[]{:S(2)}, u32[]{:S(2)}) async-start(f32[64,1,128]{2,1,0:T(1,128)} %bitcast.15), calls=%async_computation | async-start | bytes 65536 | tf_op jit(solution)/shard_map/all_to_all | solution.py:274
  15.2 0.7 %pad_add_fusion.lists_ref = s32[4,2,320]{2,1,0:T(2,128)S(1)} fusion(s32[4,2,64]{2,1,0:T(2,128)} %param.10, s32[4,2,256]{2,1,0:T(2,128)} %param.9), kind=kLoop, calls=%fused_computation | loop fusion | flops 2560 | bytes 20480 | tf_op jit(solution)/shard_map/concatenate | solution.py:298
  15.9 0.0 copy-start.1
  15.9 2.0 %shard_map.86 = (f32[8,128]{1,0:T(8,128)S(1)}, s32[8,128]{1,0:T(8,128)S(1)}, bf16[8,64,256]{2,1,0:T(8,128)(2,1)S(1)}, bf16[8,128,128]{2,1,0:T(8,128)(2,1)S(1)}) custom-call(s32[4,2,320]{2,1,0:T(2,128)S(1)} %pad_add_fusion.lists_ref, bf16[4,2,1024,128]{3,2,1,0:T(8,128)(2,1)} %key_hbm.1), custom_call_target="tpu_custom_call" | custom-call | bytes 4194304 | tf_op jit(solution)/shard_map/pallas_call | solution.py:260
  17.9 6.5 %all-to-all-done = f32[64,1,128]{2,1,0:T(1,128)S(1)} async-done(((f32[64,1,128]{2,1,0:T(1,128)}), f32[64,1,128]{2,1,0:T(1,128)S(1)}, u32[]{:S(2)}, u32[]{:S(2)}) %all-to-all-start) | async-done | bytes 32800 | tf_op jit(solution)/shard_map/all_to_all | solution.py:274
  24.4 0.0 copy-done
  24.4 0.9 %shard_map.87 = (f32[128,128]{1,0:T(8,128)S(1)}, f32[4,16,64]{2,1,0:T(8,128)S(1)}) custom-call(f32[8,128]{1,0:T(8,128)S(1)} %get-tuple-element.16.live_ref, s32[8,128]{1,0:T(8,128)S(1)} %get-tuple-element.17.start_ref, f32[64,128]{1,0:T(8,128)S(1)} %bitcast.13, bf16[8,64,256]{2,1,0:T(8,128)(2,1)S(1)} %get-tuple-element.19.ends_ref, ...), custom_call_target="tpu_custom_call" | custom-call | bytes 1048576 | tf_op jit(solution)/shard_map/pallas_call | solution.py:260
  25.3 13.8 %all_to_all.15 = f32[64,2,128]{2,1,0:T(2,128)S(1)} all-to-all(f32[64,2,128]{2,1,0:T(2,128)S(1)} %bitcast.14), channel_id=1, replica_groups=mesh['head'=4,'seq'=64] {'seq'}, dimensions={0} | all-to-all | bytes 131072 | tf_op jit(solution)/shard_map/all_to_all | solution.py:274
  39.1 0.0 copy-done.1
  39.1 0.8 %shard_map.88 = (f32[256,128]{1,0:T(8,128)S(1)}, f32[2,128]{1,0:T(2,128)S(1)}) custom-call(f32[128,128]{1,0:T(8,128)S(1)} %bitcast.11, bf16[32,8192]{1,0:T(8,128)(2,1)S(1)} %copy-done.1), custom_call_target="tpu_custom_call" | custom-call | bytes 1048576 | tf_op jit(solution)/shard_map/pallas_call | solution.py:260
  39.8 19.4 %all_to_all.16 = f32[256,1,128]{2,1,0:T(1,128)S(1)} all-to-all(f32[256,1,128]{2,1,0:T(1,128)S(1)} %bitcast.12), channel_id=1, replica_groups=mesh['head'=4,'seq'=64] {'head','seq'}, dimensions={0} | all-to-all | bytes 262144 | tf_op jit(solution)/shard_map/all_to_all | solution.py:274
  59.3 0.7 %shard_map.89 = (bf16[4,32]{1,0:T(4,128)(2,1)}, bf16[4,32]{1,0:T(4,128)(2,1)}, f32[4,16,64]{2,1,0:T(8,128)}) custom-call(f32[256,128]{1,0:T(8,128)S(1)} %bitcast.10, f32[2,128]{1,0:T(2,128)S(1)} %get-tuple-element.23.line_ref, f32[4,16,64]{2,1,0:T(8,128)S(1)} %get-tuple-element.24.bound_ref), custom_call_target="tpu_custom_call" | custom-call | bytes 262144 | tf_op jit(solution)/shard_map/pallas_call | solution.py:260
Async XLA Ops:
  2.0 22.4 %copy-start = (bf16[4,2,1024,128]{3,2,1,0:T(8,128)(2,1)S(1)}, bf16[4,2,1024,128]{3,2,1,0:T(8,128)(2,1)}, u32[]{:S(2)}) copy-start(bf16[4,2,1024,128]{3,2,1,0:T(8,128)(2,1)} %value_ref.1) | copy-start | bytes 6291460
  2.0 22.3 %all-to-all-start = ((f32[64,1,128]{2,1,0:T(1,128)}), f32[64,1,128]{2,1,0:T(1,128)S(1)}, u32[]{:S(2)}, u32[]{:S(2)}) async-start(f32[64,1,128]{2,1,0:T(1,128)} %bitcast.15), calls=%async_computation | async-start | bytes 65536 | tf_op jit(solution)/shard_map/all_to_all | solution.py:274
  15.9 23.2 %copy-start.1 = (bf16[32,8192]{1,0:T(8,128)(2,1)S(1)}, bf16[32,8192]{1,0:T(8,128)(2,1)}, u32[]{:S(2)}) copy-start(bf16[32,8192]{1,0:T(8,128)(2,1)} %weight_ref.1) | copy-start | bytes 1572868

commit v9 on v8

--- a/solution.py
+++ b/solution.py
@@ -84,6 +84,10 @@
     start_ref[...] = jnp.clip(page.astype(jnp.int32) - shard * pages, 0, pages - 1) * PAGE
     spots = pltpu.make_async_copy(start_ref, spot_ref, spot_sem)
     spots.start()
+    spots.wait()
+    starts = [
+        [pl.multiple_of(spot_ref[n, slot], PAGE) for slot in range(CAP)] for n in range(len(pairs))
+    ]
     for n in range(len(pairs)):
         key_copies[n].wait()
         for first in range(0, pages, 16):
@@ -98,11 +102,6 @@
             at = slice(first, first + 16)
             ends_ref[n, at, :dim] = jnp.concatenate(largest, axis=0).astype(jnp.bfloat16)
             ends_ref[n, at, dim:] = jnp.concatenate(smallest, axis=0).astype(jnp.bfloat16)
-    spots.wait()
-    starts = [
-        [pl.multiple_of(spot_ref[n, slot], PAGE) for slot in range(CAP)] for n in range(len(pairs))
-    ]
-    for n in range(len(pairs)):
         for slot in range(CAP):
             rows = slice(slot * PAGE, (slot + 1) * PAGE)
             keys_out[n, rows, :] = key_ref[n, pl.ds(starts[n][slot], PAGE), :]

time: 60.3 us -> 60.3 us (level)
  no operation moved by 1% of the time
where the time goes in v9:
time: 60.3 us; the launch traced here: 60 us
  blocking collectives  33.2 us (55%)
  starting transfers between devices  13.1 us (22%)
  waiting for transfers between devices  6.58 us (11%)
  Pallas kernels  5.67 us (9%)
  other arithmetic  0.72 us (1%)
  between operations  0.68 us (1%)
    all_to_all x2, blocking collectives, exchanged(): return lax.all_to_all(sent, axis, 0, 0, tiled=True).reshape(x.shape)  33.2 us
    all_to_all x1, starting transfers between devices, exchanged(): return lax.all_to_all(sent, axis, 0, 0, tiled=True).reshape(x.shape)  13.1 us
    all_to_all x1, waiting for transfers between devices, exchanged(): return lax.all_to_all(sent, axis, 0, 0, tiled=True).reshape(x.shape)  6.58 us
    pallas_call x5, Pallas kernels, call(): pl.pallas_call(kernel, out_shape=out_shape, in_specs=specs, out_specs=tup...  5.67 us
  transfers between devices with their start and end apart: 1, of which 1 were waited for; matrix products, arithmetic and copies ran while one was open for 1% of the time, Pallas kernels for 3%

profile of v9, /device:TPU:1, one launch (start us, length us, event | category | flops | bytes accessed | tf_op | source)
XLA Modules:
  0.0 60.0 jit_solution(13194794924264151754)
XLA Ops:
  0.6 1.4 %shard_map.85 = f32[64,128]{1,0:T(8,128)} custom-call(bf16[4,32]{1,0:T(4,128)(2,1)} %query_hbm.1), custom_call_target="tpu_custom_call" | custom-call | bytes 65536 | tf_op jit(solution)/shard_map/pallas_call | solution.py:259
  2.0 0.0 copy-start
  2.0 13.1 %all-to-all-start = ((f32[64,1,128]{2,1,0:T(1,128)}), f32[64,1,128]{2,1,0:T(1,128)S(1)}, u32[]{:S(2)}, u32[]{:S(2)}) async-start(f32[64,1,128]{2,1,0:T(1,128)} %bitcast.15), calls=%async_computation | async-start | bytes 65536 | tf_op jit(solution)/shard_map/all_to_all | solution.py:273
  15.2 0.7 %pad_add_fusion.lists_ref = s32[4,2,320]{2,1,0:T(2,128)S(1)} fusion(s32[4,2,64]{2,1,0:T(2,128)} %param.10, s32[4,2,256]{2,1,0:T(2,128)} %param.9), kind=kLoop, calls=%fused_computation | loop fusion | flops 2560 | bytes 20480 | tf_op jit(solution)/shard_map/concatenate | solution.py:297
  15.9 0.0 copy-start.1
  15.9 1.9 %shard_map.86 = (f32[8,128]{1,0:T(8,128)S(1)}, s32[8,128]{1,0:T(8,128)S(1)}, bf16[8,64,256]{2,1,0:T(8,128)(2,1)S(1)}, bf16[8,128,128]{2,1,0:T(8,128)(2,1)S(1)}) custom-call(s32[4,2,320]{2,1,0:T(2,128)S(1)} %pad_add_fusion.lists_ref, bf16[4,2,1024,128]{3,2,1,0:T(8,128)(2,1)} %key_hbm.1), custom_call_target="tpu_custom_call" | custom-call | bytes 4194304 | tf_op jit(solution)/shard_map/pallas_call | solution.py:259
  17.8 6.6 %all-to-all-done = f32[64,1,128]{2,1,0:T(1,128)S(1)} async-done(((f32[64,1,128]{2,1,0:T(1,128)}), f32[64,1,128]{2,1,0:T(1,128)S(1)}, u32[]{:S(2)}, u32[]{:S(2)}) %all-to-all-start) | async-done | bytes 32800 | tf_op jit(solution)/shard_map/all_to_all | solution.py:273
  24.4 0.0 copy-done
  24.4 0.9 %shard_map.87 = (f32[128,128]{1,0:T(8,128)S(1)}, f32[4,16,64]{2,1,0:T(8,128)S(1)}) custom-call(f32[8,128]{1,0:T(8,128)S(1)} %get-tuple-element.16.live_ref, s32[8,128]{1,0:T(8,128)S(1)} %get-tuple-element.17.start_ref, f32[64,128]{1,0:T(8,128)S(1)} %bitcast.13, bf16[8,64,256]{2,1,0:T(8,128)(2,1)S(1)} %get-tuple-element.19.ends_ref, ...), custom_call_target="tpu_custom_call" | custom-call | bytes 1048576 | tf_op jit(solution)/shard_map/pallas_call | solution.py:259
  25.3 13.8 %all_to_all.15 = f32[64,2,128]{2,1,0:T(2,128)S(1)} all-to-all(f32[64,2,128]{2,1,0:T(2,128)S(1)} %bitcast.14), channel_id=1, replica_groups=mesh['head'=4,'seq'=64] {'seq'}, dimensions={0} | all-to-all | bytes 131072 | tf_op jit(solution)/shard_map/all_to_all | solution.py:273
  39.1 0.0 copy-done.1
  39.1 0.8 %shard_map.88 = (f32[256,128]{1,0:T(8,128)S(1)}, f32[2,128]{1,0:T(2,128)S(1)}) custom-call(f32[128,128]{1,0:T(8,128)S(1)} %bitcast.11, bf16[32,8192]{1,0:T(8,128)(2,1)S(1)} %copy-done.1), custom_call_target="tpu_custom_call" | custom-call | bytes 1048576 | tf_op jit(solution)/shard_map/pallas_call | solution.py:259
  39.8 19.4 %all_to_all.16 = f32[256,1,128]{2,1,0:T(1,128)S(1)} all-to-all(f32[256,1,128]{2,1,0:T(1,128)S(1)} %bitcast.12), channel_id=1, replica_groups=mesh['head'=4,'seq'=64] {'head','seq'}, dimensions={0} | all-to-all | bytes 262144 | tf_op jit(solution)/shard_map/all_to_all | solution.py:273
  59.3 0.7 %shard_map.89 = (bf16[4,32]{1,0:T(4,128)(2,1)}, bf16[4,32]{1,0:T(4,128)(2,1)}, f32[4,16,64]{2,1,0:T(8,128)}) custom-call(f32[256,128]{1,0:T(8,128)S(1)} %bitcast.10, f32[2,128]{1,0:T(2,128)S(1)} %get-tuple-element.23.line_ref, f32[4,16,64]{2,1,0:T(8,128)S(1)} %get-tuple-element.24.bound_ref), custom_call_target="tpu_custom_call" | custom-call | bytes 262144 | tf_op jit(solution)/shard_map/pallas_call | solution.py:259
Async XLA Ops:
  2.0 22.4 %copy-start = (bf16[4,2,1024,128]{3,2,1,0:T(8,128)(2,1)S(1)}, bf16[4,2,1024,128]{3,2,1,0:T(8,128)(2,1)}, u32[]{:S(2)}) copy-start(bf16[4,2,1024,128]{3,2,1,0:T(8,128)(2,1)} %value_ref.1) | copy-start | bytes 6291460
  2.0 22.3 %all-to-all-start = ((f32[64,1,128]{2,1,0:T(1,128)}), f32[64,1,128]{2,1,0:T(1,128)S(1)}, u32[]{:S(2)}, u32[]{:S(2)}) async-start(f32[64,1,128]{2,1,0:T(1,128)} %bitcast.15), calls=%async_computation | async-start | bytes 65536 | tf_op jit(solution)/shard_map/all_to_all | solution.py:273
  15.9 23.2 %copy-start.1 = (bf16[32,8192]{1,0:T(8,128)(2,1)S(1)}, bf16[32,8192]{1,0:T(8,128)(2,1)}, u32[]{:S(2)}) copy-start(bf16[32,8192]{1,0:T(8,128)(2,1)} %weight_ref.1) | copy-start | bytes 1572868
